TPU v7x, 32 devices: a whole 2x2x4 slice. The times are simulated.
32 devices in a mesh: dp: 16 (over z, x, core), fsdp: 2 (over y).
Axes of the slice: x: 2, y: 2, z: 4, core: 2. Of those that a mesh axis runs over, the one named last changes fastest.
Arguments:
- hidden: bfloat16 [64, 640, 768], P(('dp', 'fsdp')), may hold values from -6 to 6
- segment_ids: int32 [64, 640], P(('dp', 'fsdp')), may hold values from 0 to 3, never falling along the last dimension, each value on 1 to 256 neighbouring positions
- token_types: int32 [64, 640], P(('dp', 'fsdp')), may hold values 0 or 1
- w_query: bfloat16 [768, 3072], P('fsdp'), may hold values from -0.21875 to 0.21875
- b_query: bfloat16 [3072], P('fsdp'), may hold values from -1.796875 to 1.796875
- w_key_value: bfloat16 [768, 1536], P('fsdp'), may hold values from -0.21875 to 0.21875
- b_value: bfloat16 [768], P('fsdp'), may hold values from -1.796875 to 1.796875
- w_output: bfloat16 [768, 768], P('fsdp'), may hold values from -0.625 to 0.625
- b_output: bfloat16 [768], P('fsdp'), may hold values from -1.796875 to 1.796875
- gain_attn: bfloat16 [768], P('fsdp'), may hold values from 0.5 to 1.5
- bias_attn: bfloat16 [768], P('fsdp'), may hold values from -1.796875 to 1.796875
- w_inner: bfloat16 [768, 3072], P('fsdp'), may hold values from -0.21875 to 0.21875
- b_inner: bfloat16 [3072], P('fsdp'), may hold values from -1.796875 to 1.796875
- w_down: bfloat16 [3072, 768], P('fsdp'), may hold values from -0.21875 to 0.21875
- b_down: bfloat16 [768], P('fsdp'), may hold values from -1.796875 to 1.796875
- gain_ffn: bfloat16 [768], P('fsdp'), may hold values from 0.5 to 1.5
- bias_ffn: bfloat16 [768], P('fsdp'), may hold values from -1.796875 to 1.796875
- cotangent: bfloat16 [64, 640, 768], P(('dp', 'fsdp')), may hold values from -6 to 6
Outputs:
- output: bfloat16 [64, 640, 768], P(('dp', 'fsdp'))
- grad_hidden: bfloat16 [64, 640, 768], P(('dp', 'fsdp'))
- grad_w_query: float32 [768, 3072], P('fsdp')
- grad_b_query: float32 [3072], P('fsdp')
- grad_w_key_value: float32 [768, 1536], P('fsdp')
- grad_b_value: float32 [768], P('fsdp')
- grad_w_output: float32 [768, 768], P('fsdp')
- grad_b_output: float32 [768], P('fsdp')
- grad_gain_attn: float32 [768], P('fsdp')
- grad_bias_attn: float32 [768], P('fsdp')
- grad_w_inner: float32 [768, 3072], P('fsdp')
- grad_b_inner: float32 [3072], P('fsdp')
- grad_w_down: float32 [3072, 768], P('fsdp')
- grad_b_down: float32 [768], P('fsdp')
- grad_gain_ffn: float32 [768], P('fsdp')
- grad_bias_ffn: float32 [768], P('fsdp')
Inputs may be any that keep to these rules, and one draw needn't show every extreme that they name: `segment_ids`: along a sequence the document number never falls; a document holds at most 256 tokens, and some document in each sequence holds exactly that many.
All inputs are finite; a program needn't handle non-finite values. No bound on the sum of `token_types` on one device may be relied on, other than what follows from the above.
Results may differ from a plain program's by a relative error of at most 0.02.
Values may be sent and summed in bfloat16 or wider, within the bound.
No kernel may reach another device: no remote copies, remote signals or barrier semaphores. Data moves between devices by JAX's collectives and lax.ppermute only.
A program may use at most 256 MiB of HBM per device.

v0:
```python
from functools import partial

import jax
import jax.numpy as jnp
from jax import lax
from jax.sharding import PartitionSpec as P

HEAD_DIM = 64


def contract_rows(left, right):
    return lax.dot_general(
        left, right, (((0,), (0,)), ((), ())), preferred_element_type=jnp.float32
    )


def times_transpose(left, right):
    return lax.dot_general(
        left, right, (((1,), (1,)), ((), ())), preferred_element_type=jnp.float32
    )


def normalize(resid, branch, gain, offset):
    summed = resid + branch
    center = summed - jnp.mean(summed, axis=-1, keepdims=True)
    spread = jnp.mean(center * center, axis=-1, keepdims=True)
    return center * lax.rsqrt(spread + 1e-05) * gain + offset


def exact_gelu(values):
    return jax.nn.gelu(values, approximate=False)


def split_heads(matrix, head_size):
    return matrix.reshape(matrix.shape[0], -1, head_size).transpose(1, 0, 2)


def merge_heads(stacked):
    return stacked.transpose(1, 0, 2).reshape(stacked.shape[1], -1)


def head_scores(key_word, same_doc, to_words, to_entities, key_rows):
    toward_words = times_transpose(to_words, key_rows)
    toward_entities = times_transpose(to_entities, key_rows)
    scores = jnp.where(key_word, toward_words, toward_entities) * key_rows.shape[-1] ** (-0.5)
    return jnp.where(same_doc, scores, -1000000000.0)


def head_forward(key_word, same_doc, pieces):
    to_words, to_entities, key_rows, value_rows = pieces
    scores = head_scores(key_word, same_doc, to_words, to_entities, key_rows)
    biggest = jnp.max(scores, axis=-1, keepdims=True)
    log_total = biggest[:, 0] + jnp.log(jnp.sum(jnp.exp(scores - biggest), axis=-1))
    probabilities = jnp.exp(scores - log_total[:, None])
    context = jnp.dot(
        probabilities.astype(jnp.bfloat16), value_rows, preferred_element_type=jnp.float32
    )
    return (context, log_total)


def head_backward(key_word, same_doc, pieces):
    to_words, to_entities, key_rows, value_rows, log_total, grad_context = pieces
    scores = head_scores(key_word, same_doc, to_words, to_entities, key_rows)
    probabilities = jnp.exp(scores - log_total[:, None])
    grad_values = contract_rows(probabilities.astype(jnp.bfloat16), grad_context)
    grad_probs = times_transpose(grad_context, value_rows)
    grad_scores = probabilities * (
        grad_probs - jnp.sum(probabilities * grad_probs, axis=-1, keepdims=True)
    )
    scaled = (grad_scores * key_rows.shape[-1] ** (-0.5)).astype(jnp.bfloat16)
    nothing = jnp.zeros_like(scaled)
    toward_words = jnp.where(key_word, scaled, nothing)
    toward_entities = jnp.where(key_word, nothing, scaled)
    grad_words = jnp.dot(toward_words, key_rows, preferred_element_type=jnp.float32)
    grad_entities = jnp.dot(toward_entities, key_rows, preferred_element_type=jnp.float32)
    grad_keys = contract_rows(toward_words, to_words) + contract_rows(toward_entities, to_entities)
    return (grad_words, grad_entities, grad_keys, grad_values)


def layer_forward(tokens, segments, kinds, gathered):
    (
        w_query,
        b_query,
        w_key_value,
        b_value,
        w_output,
        b_output,
        gain_attn,
        bias_attn,
        w_inner,
        b_inner,
        w_down,
        b_down,
        gain_ffn,
        bias_ffn,
    ) = gathered
    model_width = tokens.shape[1]
    head_size = HEAD_DIM
    is_word = (kinds == 0)[:, None]
    queries = jnp.dot(tokens, w_query, preferred_element_type=jnp.float32) + b_query.astype(
        jnp.float32
    )
    to_words = jnp.where(
        is_word, queries[:, :model_width], queries[:, 2 * model_width : 3 * model_width]
    ).astype(jnp.bfloat16)
    to_entities = jnp.where(
        is_word, queries[:, model_width : 2 * model_width], queries[:, 3 * model_width :]
    ).astype(jnp.bfloat16)
    projected = jnp.dot(tokens, w_key_value, preferred_element_type=jnp.float32)
    key_rows = projected[:, :model_width].astype(jnp.bfloat16)
    value_rows = (projected[:, model_width:] + b_value.astype(jnp.float32)).astype(jnp.bfloat16)
    key_word = (kinds == 0)[None, :]
    same_doc = segments[:, None] == segments[None, :]
    head_parts = (
        split_heads(to_words, head_size),
        split_heads(to_entities, head_size),
        split_heads(key_rows, head_size),
        split_heads(value_rows, head_size),
    )
    head_context, log_total = lax.map(partial(head_forward, key_word, same_doc), head_parts)
    context = merge_heads(head_context).astype(jnp.bfloat16)
    attended = jnp.dot(context, w_output, preferred_element_type=jnp.float32) + b_output.astype(
        jnp.float32
    )
    first_norm, first_back = jax.vjp(
        normalize,
        tokens.astype(jnp.float32),
        attended,
        gain_attn.astype(jnp.float32),
        bias_attn.astype(jnp.float32),
    )
    first_low = first_norm.astype(jnp.bfloat16)
    inner_act = jnp.dot(first_low, w_inner, preferred_element_type=jnp.float32) + b_inner.astype(
        jnp.float32
    )
    activated, gelu_back = jax.vjp(exact_gelu, inner_act)
    activated_low = activated.astype(jnp.bfloat16)
    branch = jnp.dot(activated_low, w_down, preferred_element_type=jnp.float32) + b_down.astype(
        jnp.float32
    )
    result, second_back = jax.vjp(
        normalize, first_norm, branch, gain_ffn.astype(jnp.float32), bias_ffn.astype(jnp.float32)
    )
    stash = (
        head_parts,
        log_total,
        context,
        first_low,
        activated_low,
        first_back,
        gelu_back,
        second_back,
        is_word,
        key_word,
        same_doc,
    )
    return (result.astype(jnp.bfloat16), stash)


def layer_backward(tokens, stash, gathered, incoming):
    (
        w_query,
        b_query,
        w_key_value,
        b_value,
        w_output,
        b_output,
        gain_attn,
        bias_attn,
        w_inner,
        b_inner,
        w_down,
        b_down,
        gain_ffn,
        bias_ffn,
    ) = gathered
    (
        head_parts,
        log_total,
        context,
        first_low,
        activated_low,
        first_back,
        gelu_back,
        second_back,
        is_word,
        key_word,
        same_doc,
    ) = stash
    model_width = tokens.shape[1]
    grad_first_res, grad_branch, grad_gain_ffn, grad_bias_ffn = second_back(
        incoming.astype(jnp.float32)
    )
    branch_low = grad_branch.astype(jnp.bfloat16)
    grad_b_down = jnp.sum(branch_low, axis=0, dtype=jnp.float32)
    grad_w_down = contract_rows(activated_low, branch_low)
    (grad_activated,) = gelu_back(times_transpose(branch_low, w_down))
    inner_low = grad_activated.astype(jnp.bfloat16)
    grad_b_inner = jnp.sum(inner_low, axis=0, dtype=jnp.float32)
    grad_w_inner = contract_rows(first_low, inner_low)
    grad_first = grad_first_res + times_transpose(inner_low, w_inner)
    grad_tokens_res, grad_attended, grad_gain_attn, grad_bias_attn = first_back(grad_first)
    attended_low = grad_attended.astype(jnp.bfloat16)
    grad_b_output = jnp.sum(attended_low, axis=0, dtype=jnp.float32)
    grad_w_output = contract_rows(context, attended_low)
    grad_context = times_transpose(attended_low, w_output).astype(jnp.bfloat16)
    back_parts = head_parts + (log_total, split_heads(grad_context, HEAD_DIM))
    grad_words, grad_entities, grad_keys, grad_values = lax.map(
        partial(head_backward, key_word, same_doc), back_parts
    )
    grad_words = merge_heads(grad_words)
    grad_entities = merge_heads(grad_entities)
    nothing = jnp.zeros_like(grad_words)
    grad_queries = jnp.concatenate(
        [
            jnp.where(is_word, grad_words, nothing),
            jnp.where(is_word, grad_entities, nothing),
            jnp.where(is_word, nothing, grad_words),
            jnp.where(is_word, nothing, grad_entities),
        ],
        axis=1,
    ).astype(jnp.bfloat16)
    grad_projected = jnp.concatenate(
        [merge_heads(grad_keys), merge_heads(grad_values)], axis=1
    ).astype(jnp.bfloat16)
    grad_w_query = contract_rows(tokens, grad_queries)
    grad_b_query = jnp.sum(grad_queries, axis=0, dtype=jnp.float32)
    grad_w_key_value = contract_rows(tokens, grad_projected)
    grad_b_value = jnp.sum(grad_projected[:, model_width:], axis=0, dtype=jnp.float32)
    grad_tokens = (
        grad_tokens_res
        + times_transpose(grad_queries, w_query)
        + times_transpose(grad_projected, w_key_value)
    )
    grads = [
        grad_w_query,
        grad_b_query,
        grad_w_key_value,
        grad_b_value,
        grad_w_output,
        grad_b_output,
        grad_gain_attn,
        grad_bias_attn,
        grad_w_inner,
        grad_b_inner,
        grad_w_down,
        grad_b_down,
        grad_gain_ffn,
        grad_bias_ffn,
    ]
    return (grad_tokens.astype(jnp.bfloat16), grads)


def body(
    hidden,
    segment_ids,
    token_types,
    w_query,
    b_query,
    w_key_value,
    b_value,
    w_output,
    b_output,
    gain_attn,
    bias_attn,
    w_inner,
    b_inner,
    w_down,
    b_down,
    gain_ffn,
    bias_ffn,
    cotangent,
):
    shards = (
        w_query,
        b_query,
        w_key_value,
        b_value,
        w_output,
        b_output,
        gain_attn,
        bias_attn,
        w_inner,
        b_inner,
        w_down,
        b_down,
        gain_ffn,
        bias_ffn,
    )
    group_count = lax.axis_size("fsdp")
    totals = [
        jnp.zeros((shard_piece.shape[0] * group_count,) + shard_piece.shape[1:], jnp.float32)
        for shard_piece in shards
    ]
    outputs = []
    input_grads = []
    for micro_batch in range(hidden.shape[0]):
        gathered = (
            lax.all_gather(w_query, "fsdp", axis=0, tiled=True),
            lax.all_gather(b_query, "fsdp", axis=0, tiled=True),
            lax.all_gather(w_key_value, "fsdp", axis=0, tiled=True),
            lax.all_gather(b_value, "fsdp", axis=0, tiled=True),
            lax.all_gather(w_output, "fsdp", axis=0, tiled=True),
            lax.all_gather(b_output, "fsdp", axis=0, tiled=True),
            lax.all_gather(gain_attn, "fsdp", axis=0, tiled=True),
            lax.all_gather(bias_attn, "fsdp", axis=0, tiled=True),
            lax.all_gather(w_inner, "fsdp", axis=0, tiled=True),
            lax.all_gather(b_inner, "fsdp", axis=0, tiled=True),
            lax.all_gather(w_down, "fsdp", axis=0, tiled=True),
            lax.all_gather(b_down, "fsdp", axis=0, tiled=True),
            lax.all_gather(gain_ffn, "fsdp", axis=0, tiled=True),
            lax.all_gather(bias_ffn, "fsdp", axis=0, tiled=True),
        )
        tokens = hidden[micro_batch]
        result, stash = layer_forward(
            tokens, segment_ids[micro_batch], token_types[micro_batch], gathered
        )
        gathered = (
            lax.all_gather(w_query, "fsdp", axis=0, tiled=True),
            lax.all_gather(b_query, "fsdp", axis=0, tiled=True),
            lax.all_gather(w_key_value, "fsdp", axis=0, tiled=True),
            lax.all_gather(b_value, "fsdp", axis=0, tiled=True),
            lax.all_gather(w_output, "fsdp", axis=0, tiled=True),
            lax.all_gather(b_output, "fsdp", axis=0, tiled=True),
            lax.all_gather(gain_attn, "fsdp", axis=0, tiled=True),
            lax.all_gather(bias_attn, "fsdp", axis=0, tiled=True),
            lax.all_gather(w_inner, "fsdp", axis=0, tiled=True),
            lax.all_gather(b_inner, "fsdp", axis=0, tiled=True),
            lax.all_gather(w_down, "fsdp", axis=0, tiled=True),
            lax.all_gather(b_down, "fsdp", axis=0, tiled=True),
            lax.all_gather(gain_ffn, "fsdp", axis=0, tiled=True),
            lax.all_gather(bias_ffn, "fsdp", axis=0, tiled=True),
        )
        grad_tokens, grads = layer_backward(tokens, stash, gathered, cotangent[micro_batch])
        totals = [running + update for running, update in zip(totals, grads)]
        outputs.append(result)
        input_grads.append(grad_tokens)
    shares = (
        lax.psum_scatter(
            totals[0].astype(jnp.bfloat16), "fsdp", scatter_dimension=0, tiled=True
        ).astype(jnp.float32),
        lax.psum_scatter(
            totals[1].astype(jnp.bfloat16), "fsdp", scatter_dimension=0, tiled=True
        ).astype(jnp.float32),
        lax.psum_scatter(
            totals[2].astype(jnp.bfloat16), "fsdp", scatter_dimension=0, tiled=True
        ).astype(jnp.float32),
        lax.psum_scatter(
            totals[3].astype(jnp.bfloat16), "fsdp", scatter_dimension=0, tiled=True
        ).astype(jnp.float32),
        lax.psum_scatter(
            totals[4].astype(jnp.bfloat16), "fsdp", scatter_dimension=0, tiled=True
        ).astype(jnp.float32),
        lax.psum_scatter(
            totals[5].astype(jnp.bfloat16), "fsdp", scatter_dimension=0, tiled=True
        ).astype(jnp.float32),
        lax.psum_scatter(
            totals[6].astype(jnp.bfloat16), "fsdp", scatter_dimension=0, tiled=True
        ).astype(jnp.float32),
        lax.psum_scatter(
            totals[7].astype(jnp.bfloat16), "fsdp", scatter_dimension=0, tiled=True
        ).astype(jnp.float32),
        lax.psum_scatter(
            totals[8].astype(jnp.bfloat16), "fsdp", scatter_dimension=0, tiled=True
        ).astype(jnp.float32),
        lax.psum_scatter(
            totals[9].astype(jnp.bfloat16), "fsdp", scatter_dimension=0, tiled=True
        ).astype(jnp.float32),
        lax.psum_scatter(
            totals[10].astype(jnp.bfloat16), "fsdp", scatter_dimension=0, tiled=True
        ).astype(jnp.float32),
        lax.psum_scatter(
            totals[11].astype(jnp.bfloat16), "fsdp", scatter_dimension=0, tiled=True
        ).astype(jnp.float32),
        lax.psum_scatter(
            totals[12].astype(jnp.bfloat16), "fsdp", scatter_dimension=0, tiled=True
        ).astype(jnp.float32),
        lax.psum_scatter(
            totals[13].astype(jnp.bfloat16), "fsdp", scatter_dimension=0, tiled=True
        ).astype(jnp.float32),
    )
    summed = (
        lax.psum(shares[0].astype(jnp.bfloat16), "dp").astype(jnp.float32),
        lax.psum(shares[1].astype(jnp.bfloat16), "dp").astype(jnp.float32),
        lax.psum(shares[2].astype(jnp.bfloat16), "dp").astype(jnp.float32),
        lax.psum(shares[3].astype(jnp.bfloat16), "dp").astype(jnp.float32),
        lax.psum(shares[4].astype(jnp.bfloat16), "dp").astype(jnp.float32),
        lax.psum(shares[5].astype(jnp.bfloat16), "dp").astype(jnp.float32),
        lax.psum(shares[6].astype(jnp.bfloat16), "dp").astype(jnp.float32),
        lax.psum(shares[7].astype(jnp.bfloat16), "dp").astype(jnp.float32),
        lax.psum(shares[8].astype(jnp.bfloat16), "dp").astype(jnp.float32),
        lax.psum(shares[9].astype(jnp.bfloat16), "dp").astype(jnp.float32),
        lax.psum(shares[10].astype(jnp.bfloat16), "dp").astype(jnp.float32),
        lax.psum(shares[11].astype(jnp.bfloat16), "dp").astype(jnp.float32),
        lax.psum(shares[12].astype(jnp.bfloat16), "dp").astype(jnp.float32),
        lax.psum(shares[13].astype(jnp.bfloat16), "dp").astype(jnp.float32),
    )
    return (
        jnp.stack(outputs),
        jnp.stack(input_grads),
        summed[0],
        summed[1],
        summed[2],
        summed[3],
        summed[4],
        summed[5],
        summed[6],
        summed[7],
        summed[8],
        summed[9],
        summed[10],
        summed[11],
        summed[12],
        summed[13],
    )


def solution(mesh):
    placed = (
        P(("dp", "fsdp"), None, None),
        P(("dp", "fsdp"), None),
        P(("dp", "fsdp"), None),
        P("fsdp", None),
        P("fsdp"),
        P("fsdp", None),
        P("fsdp"),
        P("fsdp", None),
        P("fsdp"),
        P("fsdp"),
        P("fsdp"),
        P("fsdp", None),
        P("fsdp"),
        P("fsdp", None),
        P("fsdp"),
        P("fsdp"),
        P("fsdp"),
        P(("dp", "fsdp"), None, None),
    )
    return jax.shard_map(
        body,
        mesh=mesh,
        in_specs=placed,
        out_specs=(
            P(("dp", "fsdp"), None, None),
            P(("dp", "fsdp"), None, None),
            P("fsdp", None),
            P("fsdp"),
            P("fsdp", None),
            P("fsdp"),
            P("fsdp", None),
            P("fsdp"),
            P("fsdp"),
            P("fsdp"),
            P("fsdp", None),
            P("fsdp"),
            P("fsdp", None),
            P("fsdp"),
            P("fsdp"),
            P("fsdp"),
        ),
        check_vma=False,
    )
```

profile of v0, /device:TPU:0, one launch (start us, length us, event | category | flops | bytes accessed | tf_op | source)
XLA Modules:
  0.0 1217.5 jit_solution(8901365981378382200)
XLA Ops:
  73.3 39.6 %all-gather.15.cloned.1.call-done = bf16[768,3072]{1,0:T(8,128)(2,1)} async-done(((bf16[384,3072]{1,0:T(8,128)(2,1)}), bf16[768,3072]{1,0:T(8,128)(2,1)}) %all-gather.15.cloned.1.call-update) | async-done | bytes 4718608 | tf_op jit(solution)/shard_map/all_gather | solution.py:299
  134.1 63.0 %while.61 = (s32[]{:T(128)}, bf16[12,640,64]{1,2,0:T(8,128)(2,1)}, f32[12,640]{1,0:T(8,128)S(1)}, pred[1,640]{1,0:T(4,128)(4,1)S(1)}, bf16[12,640,64]{2,1,0:T(8,...) while((s32[]{:T(128)}, bf16[12,640,64]{1,2,0:T(8,128)(2,1)}, ...), condition=%wide.region_11.12_spmd.clone, body=%wide.region_8.11_spmd.clone.sunk | while | flops 160972160 | bytes 9216890 | solution.py:120
  208.6 56.2 %while.60 = (s32[]{:T(128)}, bf16[12,640,64]{1,2,0:T(8,128)(2,1)S(1)}, f32[12,640]{1,0:T(8,128)S(1)}, pred[1,640]{1,0:T(4,128)(4,1)S(1)}, bf16[12,640,64]{2,1,0:...) while((s32[]{:T(128)}, ...), condition=%wide.region_3.4_spmd.clone, body=%wide.region_0.3_spmd.clone.sunk | while | flops 160972160 | bytes 9218426 | solution.py:120
  277.8 42.2 %multiply_convert_fusion.3 = (bf16[640,3072]{1,0:T(8,128)(2,1)}, f32[640,3072]{1,0:T(8,128)}, bf16[640,3072]{1,0:T(8,128)(2,1)}, f32[640,3072]{1,0:T(8,128)}, f32[640,3072]{1,0:T(8,128)}) fusion(f32[3072]{0:T(1024)S(1)} %bitcast.425, f32[640,3072]{1,0:T(8,128)S(1)} %fusion.195, bf16[768,3072]{1,0:T(8,128)(2,1)S(1)} %copy-done.100, ...), kind=kOutput, calls=%fused_computation.180 | convolution fusion | flops 3281879040 | bytes 46029824 | tf_op jit(solution)/shard_map/dot_general | solution.py:133
  320.1 7.6 fusion.216
  345.8 21.8 %convert_reduce_fusion.1 = (f32[3072]{0:T(1024)}, bf16[640,3072]{1,0:T(8,128)(2,1)}, f32[3072]{0:T(1024)}, bf16[640,3072]{1,0:T(8,128)(2,1)}) fusion(f32[640,3072]{1,0:T(8,128)} %get-tuple-element.648, f32[640,3072]{1,0:T(8,128)} %get-tuple-element.701, f32[3072]{0:T(1024)S(1)} %bitcast.426, f32[640,3072]{1,0:T(8,128)} %fusion.217, ...), kind=kOutput, calls=%fused_computation.162 | convolution fusion | flops 3086739456 | bytes 52924416 | tf_op jit(solution)/shard_map/dot_general | solution.py:18
  367.6 7.5 add_add_fusion.8
  375.1 6.2 multiply_reduce_fusion.3
  393.0 177.3 %while.62 = (s32[]{:T(128)}, bf16[12,640,64]{1,2,0:T(8,128)(2,1)}, bf16[12,640,64]{1,2,0:T(8,128)(2,1)}, bf16[12,640,64]{1,2,0:T(8,128)(2,1)}, bf16[12,640,64]{1...) while((s32[]{:T(128)}, bf16[12,640,64]{1,2,0:T(8,128)(2,1)}, ...), condition=%wide.region_22.23_spmd.clone, body=%wide.region_20.22_spmd.clone.sunk | while | flops 426024320 | bytes 19859856 | solution.py:208
  579.8 177.3 %while.63 = (s32[]{:T(128)}, bf16[12,640,64]{1,2,0:T(8,128)(2,1)}, bf16[12,640,64]{1,2,0:T(8,128)(2,1)}, bf16[12,640,64]{1,2,0:T(8,128)(2,1)}, bf16[12,640,64]{1...) while((s32[]{:T(128)}, bf16[12,640,64]{1,2,0:T(8,128)(2,1)}, ...), condition=%wide.region_29.30_spmd.clone, body=%wide.region_27.29_spmd.clone.sunk | while | flops 426024320 | bytes 19859856 | solution.py:208
  777.7 7.5 fusion.173
  785.3 9.2 fusion.140
  794.5 6.6 copy.126
  807.1 6.2 fusion.219
  820.6 6.4 fusion.197
  827.1 6.4 add_convert_fusion.1
  840.4 23.0 %reduce-scatter.16.cloned.1.call-done = bf16[384,3072]{1,0:T(8,128)(2,1)} async-done(((bf16[768,3072]{1,0:T(8,128)(2,1)}), bf16[384,3072]{1,0:T(8,128)(2,1)}) %reduce-scatter.16.cloned.1.call-update) | async-done | bytes 2359312
  867.6 20.3 %reduce-scatter.10.cloned.1.call-done = bf16[384,768]{1,0:T(8,128)(2,1)} async-done(((bf16[768,768]{1,0:T(8,128)(2,1)}), bf16[384,768]{1,0:T(8,128)(2,1)}) %reduce-scatter.10.cloned.1.call-update) | async-done | bytes 589840 | tf_op jit(solution)/shard_map/reduce_scatter | solution.py:351
  888.0 63.0 %reduce-scatter.14.cloned.1.call-done = bf16[1536,768]{1,0:T(8,128)(2,1)} async-done(((bf16[3072,768]{1,0:T(8,128)(2,1)}), bf16[1536,768]{1,0:T(8,128)(2,1)}) %reduce-scatter.14.cloned.1.call-update) | async-done | bytes 2359312 | tf_op jit(solution)/shard_map/reduce_scatter | solution.py:369
  951.0 62.8 %reduce-scatter.12.cloned.1.call-done = bf16[384,3072]{1,0:T(8,128)(2,1)} async-done(((bf16[768,3072]{1,0:T(8,128)(2,1)}), bf16[384,3072]{1,0:T(8,128)(2,1)}) %reduce-scatter.12.cloned.1.call-update) | async-done | bytes 2359312 | tf_op jit(solution)/shard_map/reduce_scatter | solution.py:363
  1018.3 7.2 all-reduce.11
  1026.2 63.2 %all-reduce.9 = (bf16[1536]{0:T(1024)(128)(2,1)S(1)}, bf16[384]{0:T(512)(128)(2,1)S(1)}, bf16[384]{0:T(512)(128)(2,1)S(1)}, bf16[384]{0:T(512)(128)(2,1)S(1)}, b...) all-reduce(bf16[1536]{0:T(1024)(128)(2,1)S(1)} %dynamic-slice.1, ...), channel_id=1, replica_groups=mesh['dp'=16,'fsdp'=2] {'dp'}, use_global_device_ids=true, to_apply=%region_35.36 | all-reduce | flops 5760 | bytes 23040 | tf_op jit(solution)/shard_map/psum | solution.py:384
  1094.6 6.6 fusion.202
  1114.5 83.1 %all-reduce.14.cloned.1.call-done = (bf16[384,3072]{0,1:T(8,128)(2,1)}, bf16[384,1536]{0,1:T(8,128)(2,1)}, bf16[384,768]{1,0:T(8,128)(2,1)}, bf16[384,3072]{1,0:T(8,128)(2,1)}, bf16[1536,768]{1,0:T(8,128)(2,1)}) async-done(((bf16[384,3072]{0,1:T(8,128)(2,1)}, bf16[384,1536]{0,1:T(8,128)(2,1)}, bf16[384,768]{1,0:T(8,128)(2,1)}, bf16[384,3072]{1,0:T(8,128)(2,1)}, bf16[1536,768]{1,0:T(8,128)(2,1)}), ...) | async-done | bytes 8847376 | tf_op jit(solution)/shard_map/psum | solution.py:383
  (881 shorter events, 702.0 us)
Async XLA Ops:
  7.2 46.0 %all-gather.17.cloned.1.call-start = ((), (), s32[]{:S(2)}) async-start(), calls=%async_computation.6 | async-start | bytes 3538944 | tf_op jit(solution)/shard_map/all_gather | solution.py:301
  7.9 105.0 %all-gather.15.cloned.1.call-start = ((), (), s32[]{:S(2)}) async-start(), calls=%async_computation.5 | async-start | bytes 7077888 | tf_op jit(solution)/shard_map/all_gather | solution.py:299
  8.7 188.4 %all-gather.19.cloned.1.call-start = ((), (), s32[]{:S(2)}) async-start(), calls=%async_computation.7 | async-start | bytes 1769472 | tf_op jit(solution)/shard_map/all_gather | solution.py:303
  9.5 15.5 %copy-start.94 = (bf16[384]{0:T(512)(128)(2,1)S(1)}, bf16[384]{0:T(512)(128)(2,1)}, u32[]{:S(2)}) copy-start(bf16[384]{0:T(512)(128)(2,1)} %param.35) | copy-start | bytes 2308
  9.5 19.9 %copy-start.95 = (bf16[384]{0:T(512)(128)(2,1)S(1)}, bf16[384]{0:T(512)(128)(2,1)}, u32[]{:S(2)}) copy-start(bf16[384]{0:T(512)(128)(2,1)} %param.36) | copy-start | bytes 2308
  9.5 24.3 %copy-start.91 = (bf16[1536]{0:T(1024)(128)(2,1)S(1)}, bf16[1536]{0:T(1024)(128)(2,1)}, u32[]{:S(2)}) copy-start(bf16[1536]{0:T(1024)(128)(2,1)} %param.38) | copy-start | bytes 9220
  9.5 28.8 %copy-start.96 = (bf16[384]{0:T(512)(128)(2,1)S(1)}, bf16[384]{0:T(512)(128)(2,1)}, u32[]{:S(2)}) copy-start(bf16[384]{0:T(512)(128)(2,1)} %param.40) | copy-start | bytes 2308
  9.5 33.8 %copy-start.97 = (bf16[384]{0:T(512)(128)(2,1)S(1)}, bf16[384]{0:T(512)(128)(2,1)}, u32[]{:S(2)}) copy-start(bf16[384]{0:T(512)(128)(2,1)} %param.41) | copy-start | bytes 2308
  9.5 38.7 %copy-start.98 = (bf16[384]{0:T(512)(128)(2,1)S(1)}, bf16[384]{0:T(512)(128)(2,1)}, u32[]{:S(2)}) copy-start(bf16[384]{0:T(512)(128)(2,1)} %param.42) | copy-start | bytes 2308
  9.5 43.7 %copy-start.103 = (bf16[2,640,768]{2,1,0:T(8,128)(2,1)S(1)}, bf16[2,640,768]{2,1,0:T(8,128)(2,1)}, u32[]{:S(2)}) copy-start(bf16[2,640,768]{2,1,0:T(8,128)(2,1)} %param.26) | copy-start | bytes 5898244
  9.5 258.9 %all-gather.21.cloned.1.call-start = ((), (), s32[]{:S(2)}) async-start(), calls=%async_computation.8 | async-start | bytes 7077888 | tf_op jit(solution)/shard_map/all_gather | solution.py:307
  10.1 310.0 %all-gather.23.cloned.1.call-start = ((), (), s32[]{:S(2)}) async-start(), calls=%async_computation.9 | async-start | bytes 7077888 | tf_op jit(solution)/shard_map/all_gather | solution.py:309
  10.7 827.3 %reduce-scatter.18.cloned.1.call-start = ((), (), s32[]{:S(2)}) async-start(), calls=%async_computation.14 | async-start | bytes 3538944
  16.1 106.2 %copy-start.83 = (pred[640]{0:T(1024)(128)(4,1)}, pred[640]{0:T(1024)(128)(4,1)S(1)}, u32[]{:S(2)}) copy-start(pred[640]{0:T(1024)(128)(4,1)S(1)} %get-tuple-element.649) | copy-start | bytes 1924
  16.1 106.2 %copy-start.85 = (pred[640]{0:T(1024)(128)(4,1)}, pred[640]{0:T(1024)(128)(4,1)S(1)}, u32[]{:S(2)}) copy-start(pred[640]{0:T(1024)(128)(4,1)S(1)} %get-tuple-element.684) | copy-start | bytes 1924
  33.8 294.4 %copy-start.65 = (f32[768]{0:T(1024)}, f32[768]{0:T(1024)S(1)}, u32[]{:S(2)}) copy-start(f32[768]{0:T(1024)S(1)} %reshape.333) | copy-start | bytes 9220
  71.5 41.4 %copy-start.104 = (bf16[2,640,768]{2,1,0:T(8,128)(2,1)S(1)}, bf16[2,640,768]{2,1,0:T(8,128)(2,1)}, u32[]{:S(2)}) copy-start(bf16[2,640,768]{2,1,0:T(8,128)(2,1)} %param.26) | copy-start | bytes 5898244
  268.0 113.4 %copy-start.2 = (f32[640,768]{1,0:T(8,128)}, f32[640,768]{1,0:T(8,128)S(1)}, u32[]{:S(2)}) copy-start(f32[640,768]{1,0:T(8,128)S(1)} %get-tuple-element.698) | copy-start | bytes 5898244
  277.8 42.3 %copy-start.89 = (f32[768]{0:T(1024)S(1)}, f32[768]{0:T(1024)}, u32[]{:S(2)}) copy-start(f32[768]{0:T(1024)} %reshape.335) | copy-start | bytes 9220
  765.5 97.9 %reduce-scatter.16.cloned.1.call-start = ((), (), s32[]{:S(2)}) async-start(), calls=%async_computation.13 | async-start | bytes 7077888
  801.1 86.9 %reduce-scatter.10.cloned.1.call-start = ((), (), s32[]{:S(2)}) async-start(), calls=%async_computation.10 | async-start | bytes 1769472 | tf_op jit(solution)/shard_map/reduce_scatter | solution.py:351
  806.9 144.1 %reduce-scatter.14.cloned.1.call-start = ((), (), s32[]{:S(2)}) async-start(), calls=%async_computation.12 | async-start | bytes 7077888 | tf_op jit(solution)/shard_map/reduce_scatter | solution.py:369
  819.0 194.8 %reduce-scatter.12.cloned.1.call-start = ((), (), s32[]{:S(2)}) async-start(), calls=%async_computation.11 | async-start | bytes 7077888 | tf_op jit(solution)/shard_map/reduce_scatter | solution.py:363
  833.6 364.0 %all-reduce.14.cloned.1.call-start = ((), (), s32[]{:S(2)}) async-start(), calls=%async_computation.15 | async-start | bytes 17694720 | tf_op jit(solution)/shard_map/psum | solution.py:383
  (103 other events, 434.4 us)
Sparse Core Ops, SparseCore 0:
  9.6 39.0 all-gather.16
  50.2 62.6 all-gather.14
  114.4 22.7 all-gather.18
  138.7 62.6 all-gather.20
  202.7 62.6 all-gather.22
  765.6 34.7 reduce-scatter.17
  803.3 59.9 reduce-scatter.15
  866.2 21.7 reduce-scatter.9
  891.0 59.9 reduce-scatter.13
  953.7 59.9 reduce-scatter.11
  1019.2 178.3 all-reduce.13
where the time goes:
time: 1230 us; the launch traced here: 1220 us
  matrix products  628 us (51%)
  waiting for transfers between devices  295 us (24%)
  local copies, waits for them, and re-layouts  110 us (9%)
  blocking collectives  110 us (9%)
  other arithmetic  53.7 us (4%)
  between operations  17.1 us (1%)
    dot_general x130, matrix products, times_transpose(): lax.dot_general(left, right, (((1,), (1,)), ((), ())), preferred_element_...  234 us
    dot_general x82, matrix products, contract_rows(): lax.dot_general(left, right, (((0,), (0,)), ((), ())), preferred_element_...  181 us
    psum x1, waiting for transfers between devices, body(): lax.psum(shares[0].astype(jnp.bfloat16), 'dp').astype(jnp.float32)  83.1 us
    psum x1, blocking collectives, body(): lax.psum(shares[1].astype(jnp.bfloat16), 'dp').astype(jnp.float32)  63.2 us
    reduce_scatter x1, waiting for transfers between devices, body(): lax.psum_scatter(totals[10].astype(jnp.bfloat16), 'fsdp', scatter_dimensi...  63 us
    reduce_scatter x1, waiting for transfers between devices, body(): lax.psum_scatter(totals[8].astype(jnp.bfloat16), 'fsdp', scatter_dimensio...  62.8 us
    unnamed x265, local copies, waits for them, and re-layouts  60.6 us
    dot_general x2, matrix products, layer_forward(): jnp.dot(first_low, w_inner, preferred_element_type=jnp.float32)  48.4 us
  transfers between devices with their start and end apart: 11, of which 6 were waited for; matrix products, arithmetic and copies ran while one was open for 26% of the time, Pallas kernels for 0%

commit v1 on v0

v1 whole, which is shorter than its diff:
```python
from functools import partial

import jax
import jax.numpy as jnp
from jax import lax
from jax.experimental import pallas as pl
from jax.experimental.pallas import tpu as pltpu
from jax.sharding import PartitionSpec as P

F32 = jnp.float32
BF = jnp.bfloat16
HEAD = 64
HEADS_PER_GROUP = 4
GROUP = HEAD * HEADS_PER_GROUP
BLOCK = 128
EXTRA = 16
EPS = 1e-05
LOG2E = 1.4426950408889634
SCALE = HEAD**-0.5
ROOT_HALF = 0.7071067811865476
INV_ROOT_2PI = 0.3989422804014327
FAR = float(2.0**33)
VMEM = 56 << 20
DP, FSDP = "dp", "fsdp"
VECTORS = range(9)
B_QUERY, B_VALUE, B_OUTPUT, GAIN_ATTN, BIAS_ATTN, B_INNER, B_DOWN, GAIN_FFN, BIAS_FFN = VECTORS
ROWS = 640


def dot(left, right, over_left=1, over_right=0):
    return lax.dot_general(
        left, right, (((over_left,), (over_right,)), ((), ())), preferred_element_type=F32
    )


def shaped(shape, dtype):
    return jax.ShapeDtypeStruct(shape, dtype)


def low_lanes(rows):
    return lax.broadcasted_iota(jnp.int32, (rows, 128), 1) < HEAD


def column_sums(values):
    return jnp.sum(values, axis=0, keepdims=True)


def row_block(rows, columns, part=0):
    return pl.BlockSpec((rows, columns), lambda i, *_: (i, part))


def whole(array):
    return pl.BlockSpec(array.shape, lambda i, *_: (0,) * array.ndim)


def settings():
    return pltpu.CompilerParams(vmem_limit_bytes=VMEM, dimension_semantics=("arbitrary",))


def cost(flops, nbytes):
    return pl.CostEstimate(flops=int(flops), bytes_accessed=int(nbytes), transcendentals=0)


def spans_of(spec, position):
    made = []
    for start, size in spec:
        if callable(start):
            start = pl.multiple_of(start(position), 16)
        made.append(pl.ds(start, size))
    return tuple(made)


def copies(position, refs, loads, targets, sems):
    made = []
    for i, (source, spec, to) in enumerate(loads):
        target = targets[i] if isinstance(targets, list) else targets
        made.append(
            pltpu.make_async_copy(
                refs[source].at[spans_of(spec, position)],
                target.at[spans_of(to, position)],
                sems.at[i],
            )
        )
    return made


def begin(made):
    for copy in made:
        copy.start()


def finish(made):
    for copy in made:
        copy.wait()


def moments(summed):
    center = summed - jnp.mean(summed, axis=-1, keepdims=True)
    inverse = lax.rsqrt(jnp.mean(center * center, axis=-1, keepdims=True) + EPS)
    return center * inverse, inverse


def norm_back(grad, hat, inverse, gain):
    scaled = grad * gain
    return inverse * (
        scaled
        - jnp.mean(scaled, axis=-1, keepdims=True)
        - hat * jnp.mean(scaled * hat, axis=-1, keepdims=True)
    )


def vector(vec_ref, spans, name):
    start, size = spans[name]
    rows = [vec_ref[i : i + 1, start : start + size] for i in range(vec_ref.shape[0])]
    return rows[0] if len(rows) == 1 else jnp.concatenate(rows, 1)


def qkv_attention(loads, spans, group, n_refs, lo_ref, n_ref, at_ref, x_ref, vec_ref, word_ref, mq_ref, mk_ref, *rest):
    refs, rest = rest[:n_refs], rest[n_refs:]
    qd_ref, kd_ref, v_ref, context_ref, log_ref, w_ref, vx_ref, sems = rest
    s = pl.program_id(0)

    @pl.when(s == 0)
    def _():
        made = copies(at_ref, refs, loads, w_ref, sems)
        begin(made)
        finish(made)

    x = x_ref[...]
    rows, width = x.shape
    blocks = rows // BLOCK
    word = word_ref[...]
    low = low_lanes(rows)
    key_mask = jnp.where(low, word, 1.0 - word)
    is_word = jnp.concatenate([word] * (GROUP // 128), 1) > 0.5

    def project(part, name, at):
        made = dot(x, w_ref[:, part * GROUP : (part + 1) * GROUP])
        if name is None:
            return made
        start = at + group * GROUP
        return made + vector(vec_ref, spans, name)[:, start : start + GROUP]

    to_words = jnp.where(
        is_word, project(0, B_QUERY, 0), project(2, B_QUERY, 2 * width)
    )
    to_entities = jnp.where(
        is_word, project(1, B_QUERY, width), project(3, B_QUERY, 3 * width)
    )
    keys = project(4, None, 0).astype(BF).astype(F32)
    vals = project(5, B_VALUE, 0).astype(BF)
    v_ref[...] = vals
    for p in range(GROUP // 128):
        lanes = slice(128 * p, 128 * p + 128)
        a, e, k = to_words[:, lanes], to_entities[:, lanes], keys[:, lanes]
        first, second = slice(256 * p, 256 * p + 128), slice(256 * p + 128, 256 * p + 256)
        qd_ref[:, first] = jnp.where(low, a, pltpu.roll(e, 64, 1)).astype(BF)
        qd_ref[:, second] = jnp.where(low, pltpu.roll(a, 64, 1), e).astype(BF)
        turned = pltpu.roll(k, 64, 1)
        kd_ref[:, first] = (jnp.where(low, k, turned) * key_mask).astype(BF)
        kd_ref[:, second] = (jnp.where(low, turned, k) * key_mask).astype(BF)
        v = vals[:, lanes].astype(F32)
        zero, one = jnp.zeros_like(v), jnp.ones_like(v)
        vx_ref[p, 0] = jnp.concatenate(
            [jnp.where(low, v, zero), jnp.where(low, one, zero)], 1
        ).astype(BF)
        vx_ref[p, 1] = jnp.concatenate(
            [jnp.where(low, zero, v), jnp.where(low, zero, one)], 1
        ).astype(BF)
    low_block = low_lanes(BLOCK)

    def query_block(i, carry):
        lo, n = lo_ref[s, i], n_ref[s, i]
        q_at = pl.ds(pl.multiple_of(i * BLOCK, BLOCK), BLOCK)
        for nk in range(1, blocks + 1):

            @pl.when(n == nk)
            def _(nk=nk):
                k_at = pl.ds(pl.multiple_of(lo * BLOCK, BLOCK), nk * BLOCK)
                mq, mk = mq_ref[q_at, :], mk_ref[k_at, :]
                logs = []
                for p in range(GROUP // 128):
                    parts, tops = [], []
                    for h in (2 * p, 2 * p + 1):
                        q = jnp.concatenate([qd_ref[q_at, 128 * h : 128 * h + 128], mq], 1)
                        k = jnp.concatenate([kd_ref[k_at, 128 * h : 128 * h + 128], mk], 1)
                        scores = dot(q, k, 1, 1)
                        top = jnp.max(scores, axis=1, keepdims=True)
                        parts.append(jnp.exp2((scores - top) * (LOG2E * SCALE)).astype(BF))
                        tops.append(top)
                    v = jnp.concatenate([vx_ref[p, 0, k_at, :], vx_ref[p, 1, k_at, :]], 0)
                    made = dot(jnp.concatenate(parts, 1), v)
                    total = made[:, 128:]
                    context_ref[q_at, 128 * p : 128 * p + 128] = (made[:, :128] / total).astype(BF)
                    top = jnp.where(low_block, tops[0], tops[1])
                    log_total = jnp.transpose(top * (LOG2E * SCALE) + jnp.log2(total))
                    logs += [log_total[0:1], log_total[64:65]]
                logs.append(jnp.zeros((8 - HEADS_PER_GROUP, 128), F32))
                log_ref[0, i] = jnp.concatenate(logs, 0)

        return carry

    lax.fori_loop(0, blocks, query_block, 0)


def call_qkv_attention(group, lo, n, at, x, vec, spans, word, mq, mk, refs, loads):
    tokens, width = x.shape
    seqs, blocks = lo.shape
    length = tokens // seqs
    return pl.pallas_call(
        partial(qkv_attention, loads, spans, group, len(refs)),
        out_shape=[
            shaped((tokens, 2 * GROUP), BF),
            shaped((tokens, 2 * GROUP), BF),
            shaped((tokens, GROUP), BF),
            shaped((tokens, GROUP), BF),
            shaped((seqs, blocks, 8, 128), F32),
        ],
        grid_spec=pltpu.PrefetchScalarGridSpec(
            num_scalar_prefetch=3,
            grid=(seqs,),
            in_specs=[row_block(length, width), whole(vec)]
            + [row_block(length, 128)] * 3
            + [pl.BlockSpec(memory_space=pl.ANY)] * len(refs),
            out_specs=[
                row_block(length, 2 * GROUP),
                row_block(length, 2 * GROUP),
                row_block(length, GROUP),
                row_block(length, GROUP),
                pl.BlockSpec((1, blocks, 8, 128), lambda i, *_: (i, 0, 0, 0)),
            ],
            scratch_shapes=[
                pltpu.VMEM((width, 6 * GROUP), BF),
                pltpu.VMEM((GROUP // 128, 2, length, 256), BF),
                pltpu.SemaphoreType.DMA((len(loads),)),
            ],
        ),
        compiler_params=settings(),
        cost_estimate=cost(6e9, 12 << 20),
        name="qkv_attention",
    )(lo, n, at, x, vec, word, mq, mk, *refs)


def attention_back(lo_ref, n_ref, qd_ref, kd_ref, v_ref, context_ref, gc_ref, log_ref, word_ref, mq_ref, mk_ref, out_ref, gq_ref, gx_ref, dots_ref):
    s = pl.program_id(0)
    rows = v_ref.shape[0]
    blocks = rows // BLOCK
    low, low_block = low_lanes(rows), low_lanes(BLOCK)
    gq_ref[...] = jnp.zeros_like(gq_ref)
    for p in range(GROUP // 128):
        lanes = slice(128 * p, 128 * p + 128)
        g = gc_ref[:, lanes].astype(F32)
        zero = jnp.zeros_like(g)
        gx_ref[p, 0] = jnp.where(low, g, zero).astype(BF)
        gx_ref[p, 1] = jnp.where(low, zero, g).astype(BF)
        product = g * context_ref[:, lanes].astype(F32)
        for i in range(blocks):
            turned = jnp.transpose(product[i * BLOCK : (i + 1) * BLOCK])
            dots_ref[i, 2 * p : 2 * p + 1] = column_sums(turned[:64])
            dots_ref[i, 2 * p + 1 : 2 * p + 2] = column_sums(turned[64:])

    def corner(first, second):
        zero = jnp.zeros_like(first)
        return jnp.concatenate(
            [jnp.concatenate([first, zero], 1), jnp.concatenate([zero, second], 1)], 0
        )

    def key_block(j, carry):
        lo, n = lo_ref[s, j], n_ref[s, j]
        k_at = pl.ds(pl.multiple_of(j * BLOCK, BLOCK), BLOCK)
        for nq in range(1, blocks + 1):

            @pl.when(n == nq)
            def _(nq=nq):
                q_at = pl.ds(pl.multiple_of(lo * BLOCK, BLOCK), nq * BLOCK)
                mq, mk = mq_ref[q_at, :], mk_ref[k_at, :]
                word = word_ref[k_at, :]
                key_mask = jnp.where(low_block, word, 1.0 - word) * SCALE
                logs = [log_ref[0, lo + t] for t in range(nq)]
                dots = [dots_ref[lo + t] for t in range(nq)]
                for p in range(GROUP // 128):
                    lanes = slice(128 * p, 128 * p + 128)
                    v = v_ref[k_at, lanes]
                    probs, grads, qs, ks = [], [], [], []
                    for half in range(2):
                        h = 2 * p + half
                        q = qd_ref[q_at, 128 * h : 128 * h + 128]
                        k = kd_ref[k_at, 128 * h : 128 * h + 128]
                        qs.append(q)
                        ks.append(k)
                        scores = dot(
                            jnp.concatenate([k, mk], 1), jnp.concatenate([q, mq], 1), 1, 1
                        )
                        log_row = jnp.concatenate([a[h : h + 1] for a in logs], 1)
                        dot_row = jnp.concatenate([a[h : h + 1] for a in dots], 1)
                        prob = jnp.exp2(scores * (LOG2E * SCALE) - log_row)
                        grad_prob = dot(v, gx_ref[p, half, q_at, :], 1, 1)
                        probs.append(prob.astype(BF))
                        grads.append((prob * (grad_prob - dot_row)).astype(BF))
                    grad_v = dot(
                        jnp.concatenate(probs, 1),
                        jnp.concatenate([gx_ref[p, 0, q_at, :], gx_ref[p, 1, q_at, :]], 0),
                    )
                    grad_k = dot(jnp.concatenate(grads, 1), corner(*qs))
                    a, b = grad_k[:, :128] * key_mask, grad_k[:, 128:] * key_mask
                    a, b = a + pltpu.roll(a, 64, 1), b + pltpu.roll(b, 64, 1)
                    at = 4 * GROUP + 128 * p
                    out_ref[k_at, at : at + 128] = jnp.where(low_block, a, b).astype(BF)
                    at = 5 * GROUP + 128 * p
                    out_ref[k_at, at : at + 128] = grad_v.astype(BF)
                    gq_ref[q_at, 256 * p : 256 * p + 256] += dot(
                        jnp.concatenate(grads, 0), corner(*ks), 0, 0
                    )

        return carry

    lax.fori_loop(0, blocks, key_block, 0)
    word = word_ref[...]
    entity = 1.0 - word
    for p in range(GROUP // 128):
        a = gq_ref[:, 256 * p : 256 * p + 128] * SCALE
        b = gq_ref[:, 256 * p + 128 : 256 * p + 256] * SCALE
        to_words = jnp.where(low, a, pltpu.roll(b, 64, 1))
        to_entities = jnp.where(low, pltpu.roll(a, 64, 1), b)
        made = (to_words * word, to_entities * word, to_words * entity, to_entities * entity)
        for part, value in enumerate(made):
            at = part * GROUP + 128 * p
            out_ref[:, at : at + 128] = value.astype(BF)


def call_attention_back(group, lo, n, kept, grad_context, word, mq, mk):
    qd, kd, v, context, log_total = kept
    tokens = v.shape[0]
    seqs, blocks = lo.shape
    length = tokens // seqs
    return pl.pallas_call(
        attention_back,
        out_shape=shaped((tokens, 6 * GROUP), BF),
        grid_spec=pltpu.PrefetchScalarGridSpec(
            num_scalar_prefetch=2,
            grid=(seqs,),
            in_specs=[
                row_block(length, 2 * GROUP),
                row_block(length, 2 * GROUP),
                row_block(length, GROUP),
                row_block(length, GROUP),
                row_block(length, GROUP, group),
                pl.BlockSpec((1, blocks, 8, 128), lambda i, *_: (i, 0, 0, 0)),
            ]
            + [row_block(length, 128)] * 3,
            out_specs=row_block(length, 6 * GROUP),
            scratch_shapes=[
                pltpu.VMEM((length, 2 * GROUP), F32),
                pltpu.VMEM((GROUP // 128, 2, length, 128), BF),
                pltpu.VMEM((blocks, 8, 128), F32),
            ],
        ),
        compiler_params=settings(),
        cost_estimate=cost(6e9, 12 << 20),
        name="attention_back",
    )(lo, n, qd, kd, v, context, grad_context, log_total, word, mq, mk)


def output_norm_inner(loads, spans, n_refs, n_parts, at_ref, x_ref, vec_ref, *rest):
    parts, rest = rest[:n_parts], rest[n_parts:]
    refs, rest = rest[:n_refs], rest[n_refs:]
    context_ref, hat_ref, inverse_ref, low_ref, act_ref, slope_ref, wo_ref, wi_ref, so, si = rest
    load_o = partial(copies, at_ref, refs, loads[0], wo_ref, so)
    load_i = partial(copies, at_ref, refs, loads[1], wi_ref, si)
    first = pl.program_id(0) == 0

    @pl.when(first)
    def _():
        made = load_o()
        begin(made)
        begin(load_i())
        finish(made)

    take = partial(vector, vec_ref, spans)
    context = jnp.concatenate([part[...] for part in parts], 1)
    context_ref[...] = context
    attended = dot(context, wo_ref[...]) + take(B_OUTPUT)
    hat, inverse = moments(x_ref[...].astype(F32) + attended)
    hat_ref[...] = hat
    inverse_ref[...] = jnp.broadcast_to(inverse, inverse_ref.shape)
    low = (hat * take(GAIN_ATTN) + take(BIAS_ATTN)).astype(BF)
    low_ref[...] = low

    @pl.when(first)
    def _():
        finish(load_i())

    hidden = wi_ref.shape[1]
    step = 512
    b_inner = take(B_INNER)
    for start in range(0, hidden, step):
        lanes = slice(start, start + step)
        inner = dot(low, wi_ref[:, lanes]) + b_inner[:, lanes]
        below = 0.5 * lax.erf(inner * ROOT_HALF) + 0.5
        act_ref[:, lanes] = (inner * below).astype(BF)
        bell = INV_ROOT_2PI * jnp.exp(-0.5 * inner * inner)
        slope_ref[:, lanes] = (below + inner * bell).astype(BF)


def call_output_norm_inner(at, parts, x, vec, spans, refs, loads, hidden):
    tokens, width = x.shape
    rows = ROWS
    return pl.pallas_call(
        partial(output_norm_inner, loads, spans, len(refs), len(parts)),
        out_shape=[
            shaped((tokens, width), BF),
            shaped((tokens, width), F32),
            shaped((tokens, 128), F32),
            shaped((tokens, width), BF),
            shaped((tokens, hidden), BF),
            shaped((tokens, hidden), BF),
        ],
        grid_spec=pltpu.PrefetchScalarGridSpec(
            num_scalar_prefetch=1,
            grid=(tokens // rows,),
            in_specs=[row_block(rows, width), whole(vec)]
            + [row_block(rows, GROUP)] * len(parts)
            + [pl.BlockSpec(memory_space=pl.ANY)] * len(refs),
            out_specs=[
                row_block(rows, width),
                row_block(rows, width),
                row_block(rows, 128),
                row_block(rows, width),
                row_block(rows, hidden),
                row_block(rows, hidden),
            ],
            scratch_shapes=[
                pltpu.VMEM((width, width), BF),
                pltpu.VMEM((width, hidden), BF),
                pltpu.SemaphoreType.DMA((len(loads[0]),)),
                pltpu.SemaphoreType.DMA((len(loads[1]),)),
            ],
        ),
        compiler_params=settings(),
        cost_estimate=cost(2 * tokens * width * (width + hidden), 30 << 20),
        name="output_norm_inner",
    )(at, x, vec, *parts, *refs)


def down_norm(loads, spans, n_refs, at_ref, act_ref, hat_ref, g_ref, vec_ref, *rest):
    refs, rest = rest[:n_refs], rest[n_refs:]
    out_ref, sum_ref, low_ref, small_ref, wd_ref, sd = rest

    @pl.when(pl.program_id(0) == 0)
    def _():
        made = copies(at_ref, refs, loads[2], wd_ref, sd)
        begin(made)
        small_ref[...] = jnp.zeros_like(small_ref)
        finish(made)

    take = partial(vector, vec_ref, spans)
    branch = dot(act_ref[...], wd_ref[...]) + take(B_DOWN)
    first = hat_ref[...] * take(GAIN_ATTN) + take(BIAS_ATTN)
    hat, inverse = moments(first + branch)
    out_ref[...] = (hat * take(GAIN_FFN) + take(BIAS_FFN)).astype(BF)
    g = g_ref[...].astype(F32)
    grad = norm_back(g, hat, inverse, take(GAIN_FFN))
    sum_ref[...] = grad
    low = grad.astype(BF)
    low_ref[...] = low
    small_ref[0:1] += column_sums(g * hat)
    small_ref[1:2] += column_sums(g)
    small_ref[2:3] += column_sums(low.astype(F32))


def call_down_norm(at, act, hat, g, vec, spans, refs, loads):
    tokens, width = hat.shape
    hidden = act.shape[1]
    rows = ROWS
    return pl.pallas_call(
        partial(down_norm, loads, spans, len(refs)),
        out_shape=[
            shaped((tokens, width), BF),
            shaped((tokens, width), F32),
            shaped((tokens, width), BF),
            shaped((8, width), F32),
        ],
        grid_spec=pltpu.PrefetchScalarGridSpec(
            num_scalar_prefetch=1,
            grid=(tokens // rows,),
            in_specs=[row_block(rows, hidden), row_block(rows, width), row_block(rows, width), whole(vec)]
            + [pl.BlockSpec(memory_space=pl.ANY)] * len(refs),
            out_specs=[
                row_block(rows, width),
                row_block(rows, width),
                row_block(rows, width),
                pl.BlockSpec((8, width), lambda i, *_: (0, 0)),
            ],
            scratch_shapes=[
                pltpu.VMEM((hidden, width), BF),
                pltpu.SemaphoreType.DMA((len(loads[2]),)),
            ],
        ),
        compiler_params=settings(),
        cost_estimate=cost(2 * tokens * width * hidden, 20 << 20),
        name="down_norm",
    )(at, act, hat, g, vec, *refs)


def inner_back(loads, spans, n_refs, at_ref, gb_ref, slope_ref, sum_ref, hat_ref, inverse_ref, vec_ref, *rest):
    refs, rest = rest[:n_refs], rest[n_refs:]
    gi_ref, gx_ref, ga_ref, gc_ref, small_ref, wo_ref, wi_ref, wd_ref, so, si, sd = rest
    load_o = partial(copies, at_ref, refs, loads[0], wo_ref, so)
    load_i = partial(copies, at_ref, refs, loads[1], wi_ref, si)
    load_d = partial(copies, at_ref, refs, loads[2], wd_ref, sd)
    start = pl.program_id(0) == 0

    @pl.when(start)
    def _():
        made = load_d()
        begin(made)
        begin(load_i())
        begin(load_o())
        small_ref[...] = jnp.zeros_like(small_ref)
        finish(made)

    gb = gb_ref[...]
    hidden = wi_ref.shape[1]
    step = 512
    for at in range(0, hidden, step):
        lanes = slice(at, at + step)
        grad = dot(gb, wd_ref[lanes, :], 1, 1) * slope_ref[:, lanes].astype(F32)
        gi_ref[:, lanes] = grad.astype(BF)

    @pl.when(start)
    def _():
        finish(load_i())

    grad_first = sum_ref[...] + dot(gi_ref[...], wi_ref[...], 1, 1)
    hat = hat_ref[...]
    grad = norm_back(grad_first, hat, inverse_ref[:, :1], vector(vec_ref, spans, GAIN_ATTN))
    gx_ref[...] = grad
    low = grad.astype(BF)
    ga_ref[...] = low
    small_ref[0:1] += column_sums(grad_first * hat)
    small_ref[1:2] += column_sums(grad_first)
    small_ref[2:3] += column_sums(low.astype(F32))

    @pl.when(start)
    def _():
        finish(load_o())

    gc_ref[...] = dot(low, wo_ref[...], 1, 1).astype(BF)


def call_inner_back(at, gb, slope, summed, hat, inverse, vec, spans, refs, loads):
    tokens, width = hat.shape
    hidden = slope.shape[1]
    rows = BACK_ROWS
    return pl.pallas_call(
        partial(inner_back, loads, spans, len(refs)),
        out_shape=[
            shaped((tokens, hidden), BF),
            shaped((tokens, width), F32),
            shaped((tokens, width), BF),
            shaped((tokens, width), BF),
            shaped((8, width), F32),
        ],
        grid_spec=pltpu.PrefetchScalarGridSpec(
            num_scalar_prefetch=1,
            grid=(tokens // rows,),
            in_specs=[
                row_block(rows, width),
                row_block(rows, hidden),
                row_block(rows, width),
                row_block(rows, width),
                row_block(rows, 128),
                whole(vec),
            ]
            + [pl.BlockSpec(memory_space=pl.ANY)] * len(refs),
            out_specs=[
                row_block(rows, hidden),
                row_block(rows, width),
                row_block(rows, width),
                row_block(rows, width),
                pl.BlockSpec((8, width), lambda i, *_: (0, 0)),
            ],
            scratch_shapes=[
                pltpu.VMEM((width, width), BF),
                pltpu.VMEM((width, hidden), BF),
                pltpu.VMEM((hidden, width), BF),
            ]
            + [pltpu.SemaphoreType.DMA((len(load),)) for load in loads],
        ),
        compiler_params=settings(),
        cost_estimate=cost(2 * tokens * width * (width + 2 * hidden), 30 << 20),
        name="inner_back",
    )(at, gb, slope, summed, hat, inverse, vec, *refs)


def sides(c):
    return (1 - c, c)


def down_grad(pos_ref, left_ref, right_ref, send_ref, keep_ref):
    half = right_ref.shape[1] // 2
    for out_ref, side in zip((send_ref, keep_ref), sides(pos_ref[1])):
        lanes = pl.ds(pl.multiple_of(side * half, 128), half)
        out_ref[0] = dot(left_ref[...], right_ref[:, lanes], 0, 0).astype(BF)


def call_down_grad(pos, left, right):
    tokens, rows = left.shape
    columns = right.shape[1]
    quarter = rows // 4

    def block(i, pos):
        y, x = pos[0], pos[2]
        return (0, jnp.where(i < 2, 1 - y, y) * 2 + jnp.where(i % 2 == 0, 1 - x, x))

    return pl.pallas_call(
        down_grad,
        out_shape=[shaped((2, rows // 2, columns // 2), BF)] * 2,
        grid_spec=pltpu.PrefetchScalarGridSpec(
            num_scalar_prefetch=1,
            grid=(4,),
            in_specs=[pl.BlockSpec((tokens, quarter), block), whole(right)],
            out_specs=[pl.BlockSpec((1, quarter, columns // 2), lambda i, pos: (i // 2, i % 2, 0))] * 2,
        ),
        compiler_params=settings(),
        cost_estimate=cost(1.3e10, 12 << 20),
        name="down_grad",
    )(pos, left, right)


def grad_parts(pos_ref, left_ref, right_ref, out_refs, extras):
    rows = left_ref.shape[1]
    quarter = right_ref.shape[1] // 4
    c, x = pos_ref[1], pos_ref[2]
    for out_ref, side in zip(out_refs, sides(c)):
        for k, part in enumerate(sides(x)):
            index = 2 * side + part
            lanes = pl.ds(pl.multiple_of(index * quarter, 128), quarter)
            to = slice(k * quarter, (k + 1) * quarter)
            right = right_ref[:, lanes]
            out_ref[0, :rows, to] = dot(left_ref[...], right, 0, 0).astype(BF)
            lines = [column_sums(right.astype(F32))] + extras(index)
            lines.append(jnp.zeros((EXTRA - len(lines), quarter), F32))
            out_ref[0, rows : rows + EXTRA, to] = jnp.concatenate(lines, 0).astype(BF)


def projection_grad(pos_ref, left_ref, right_ref, send_ref, keep_ref):
    grad_parts(pos_ref, left_ref, right_ref, (send_ref, keep_ref), lambda index: [])


def inner_output_grad(pos_ref, left_ref, right_ref, context_ref, ga_ref, small_a, small_b, send_ref, keep_ref, held_ref):
    vectors = [small_a[i : i + 1] for i in range(3)] + [small_b[i : i + 1] for i in range(3)]
    vectors += [jnp.zeros_like(vectors[0])] * 2

    def extras(index):
        made = []
        for first in (0, 4):
            line = vectors[first]
            for k in range(1, 4):
                line = jnp.where(index == k, vectors[first + k], line)
            made.append(line)
        return made

    outs = (send_ref, keep_ref)
    grad_parts(pos_ref, left_ref, right_ref, outs, extras)
    rows = left_ref.shape[1]
    eighth, half = rows // 4, ga_ref.shape[1] // 2
    for out_ref, side in zip(outs, sides(pos_ref[1])):
        lanes = pl.ds(pl.multiple_of(side * half, 128), half)
        held_ref[...] = dot(context_ref[...], ga_ref[:, lanes], 0, 0).astype(BF)
        for k, part in enumerate(sides(pos_ref[2])):
            for i in range(2):
                at = pl.ds(pl.multiple_of((2 * part + i) * eighth, 16), eighth)
                to = (2 * k + i) * half
                out_ref[0, rows + EXTRA :, to : to + half] = held_ref[at, :]


def call_projection_grad(pos, left, right, more=()):
    tokens, rows = left.shape
    columns = right.shape[1]
    half = rows // 2
    out_rows = half + EXTRA + (half // 4 if more else 0)
    left_block = pl.BlockSpec((tokens, half), lambda i, pos: (0, jnp.where(i == 0, 1 - pos[0], pos[0])))
    specs, scratch = [left_block, whole(right)], []
    if more:
        specs += [left_block] + [whole(m) for m in more[1:]]
        scratch = [pltpu.VMEM((half, more[1].shape[1] // 2), BF)]
    return pl.pallas_call(
        inner_output_grad if more else projection_grad,
        out_shape=[shaped((2, out_rows, columns // 2), BF)] * 2,
        grid_spec=pltpu.PrefetchScalarGridSpec(
            num_scalar_prefetch=1,
            grid=(2,),
            in_specs=specs,
            out_specs=[pl.BlockSpec((1, out_rows, columns // 2), lambda i, pos: (i, 0, 0))] * 2,
            scratch_shapes=scratch,
        ),
        compiler_params=settings(),
        cost_estimate=cost(1.8e10 if more else 9e9, 12 << 20),
        name="projection_grad",
    )(pos, left, right, *more)


def plus(*terms):
    total = terms[0].astype(F32)
    for term in terms[1:]:
        total = total + term.astype(F32)
    return total.astype(BF)


def small_call(kernel, name, pos, inputs, shapes):
    return pl.pallas_call(
        kernel,
        out_shape=[shaped(shape, dtype) for shape, dtype in shapes],
        in_specs=[pl.BlockSpec(memory_space=pltpu.SMEM)]
        + [pl.BlockSpec(memory_space=pltpu.VMEM)] * len(inputs),
        out_specs=[pl.BlockSpec(memory_space=pltpu.VMEM)] * len(shapes),
        compiler_params=pltpu.CompilerParams(vmem_limit_bytes=VMEM),
        cost_estimate=cost(3e9, 4 << 20),
        name=name,
    )(pos, *inputs)


def corners(pos_ref):
    c, x = pos_ref[1], pos_ref[2]
    return ((c, x), (c, 1 - x), (1 - c, x), (1 - c, 1 - x))


def join_down(pos_ref, *rest):
    out_ref = rest[4]
    for ref, (c, x) in zip(rest[:4], corners(pos_ref)):
        rows, columns = ref.shape
        at = pl.ds(pl.multiple_of(x * rows, 16), rows)
        out_ref[at, pl.ds(pl.multiple_of(c * columns, 128), columns)] = ref[...].astype(F32)


def join_inner(pos_ref, *rest):
    out_ref, output_ref, extra_ref = rest[4:]
    for ref, (c, x) in zip(rest[:4], corners(pos_ref)):
        columns = ref.shape[1]
        rows = out_ref.shape[0]
        lanes = pl.ds(pl.multiple_of((2 * c + x) * columns, 128), columns)
        out_ref[:, lanes] = ref[:rows, :].astype(F32)
        extra_ref[:, lanes] = ref[rows : rows + EXTRA, :].astype(F32)
        eighth, half = rows // 4, columns // 2
        for i in range(2):
            at = pl.ds(pl.multiple_of((2 * x + i) * eighth, 16), eighth)
            to = pl.ds(pl.multiple_of(c * half, 128), half)
            output_ref[at, to] = ref[rows + EXTRA :, i * half : (i + 1) * half].astype(F32)


def join_groups(n_pieces, pos_ref, *rest):
    wide_ref, parts, outs = rest[0], rest[1 : 1 + 4 * n_pieces], rest[1 + 4 * n_pieces :]
    query_ref, key_value_ref, small_ref, extra_ref = outs
    width = GROUP * n_pieces
    rows = query_ref.shape[0]
    mine = 2 * pos_ref[1] + pos_ref[2]
    for case in range(4):

        @pl.when(mine == case)
        def _(case=case):
            for piece in range(n_pieces):
                for k in range(4):
                    ref = parts[4 * piece + k]
                    columns = ref.shape[1]
                    start = (case ^ k) * columns
                    extra_ref[piece, :, start : start + columns] = ref[rows:, :].astype(F32)
                    for at in range(0, columns, 128):
                        block, more = divmod(start + at, GROUP)
                        to = query_ref if block < 4 else key_value_ref
                        first = block % 4 * width + piece * GROUP + more
                        to[:, first : first + 128] = ref[:rows, at : at + 128].astype(F32)

    late = [extra_ref[k, 0:1, :] for k in range(n_pieces)]
    query = jnp.concatenate(
        [row[:, k * GROUP : (k + 1) * GROUP] for k in range(4) for row in late], 1
    )
    value = jnp.concatenate([row[:, 5 * GROUP :] for row in late], 1)
    early = [wide_ref[1 + i : 2 + i, k * width : (k + 1) * width] for i in range(2) for k in range(4)]
    gain_ffn, bias_ffn, b_down, gain_attn, bias_attn, b_output = early[:6]
    wide = wide_ref[0:1, :]
    order = (query, value, b_output, gain_attn, bias_attn, wide, b_down, gain_ffn, bias_ffn)
    lower = jnp.concatenate([v[:, : v.shape[1] // 2] for v in order], 1)
    upper = jnp.concatenate([v[:, v.shape[1] // 2 :] for v in order], 1)
    small_ref[...] = jnp.where(pos_ref[0] == 0, lower, upper)


def pack_kernel(loads, n_refs, n_outs, pos_ref, *rest):
    refs, outs, sems = rest[:n_refs], rest[n_refs : n_refs + n_outs], rest[-1]
    made = copies(
        pos_ref, refs, [load[:3] for load in loads], [outs[load[3]] for load in loads], sems
    )
    begin(made)
    finish(made)


def call_pack(pos, refs, shapes, loads):
    return pl.pallas_call(
        partial(pack_kernel, loads, len(refs), len(shapes)),
        out_shape=[shaped(shape, BF) for shape in shapes],
        in_specs=[pl.BlockSpec(memory_space=pltpu.SMEM)]
        + [pl.BlockSpec(memory_space=pl.ANY)] * len(refs),
        out_specs=[pl.BlockSpec(memory_space=pltpu.VMEM)] * len(shapes),
        scratch_shapes=[pltpu.SemaphoreType.DMA((len(loads),))],
        compiler_params=pltpu.CompilerParams(vmem_limit_bytes=VMEM),
        cost_estimate=cost(2e9, 2 << 20),
        name="pack",
    )(pos, *refs)


def token_grad(loads, n_refs, at_ref, sum_ref, part_ref, *rest):
    refs, rest = rest[:n_refs], rest[n_refs:]
    out_ref, w_ref, sems = rest

    @pl.when(pl.program_id(0) == 0)
    def _():
        made = copies(at_ref, refs, loads, w_ref, sems)
        begin(made)
        finish(made)

    out_ref[...] = (sum_ref[...] + dot(part_ref[...], w_ref[...], 1, 1)).astype(out_ref.dtype)


def call_token_grad(at, part, summed, refs, loads, kind):
    tokens, width = summed.shape
    columns = part.shape[1]
    rows = ROWS
    return pl.pallas_call(
        partial(token_grad, loads, len(refs)),
        out_shape=shaped((tokens, width), kind),
        grid_spec=pltpu.PrefetchScalarGridSpec(
            num_scalar_prefetch=1,
            grid=(tokens // rows,),
            in_specs=[row_block(rows, width), row_block(rows, columns)]
            + [pl.BlockSpec(memory_space=pl.ANY)] * len(refs),
            out_specs=row_block(rows, width),
            scratch_shapes=[
                pltpu.VMEM((width, columns), BF),
                pltpu.SemaphoreType.DMA((len(loads),)),
            ],
        ),
        compiler_params=settings(),
        cost_estimate=cost(8e9, 12 << 20),
        name="token_grad",
    )(at, summed, part, *refs)


def document_facts(segments, kinds):
    seqs, length = segments.shape
    tokens = seqs * length
    first, last = segments[:, ::BLOCK], segments[:, BLOCK - 1 :: BLOCK]
    meets = jnp.logical_and(
        first[:, :, None] <= last[:, None, :], first[:, None, :] <= last[:, :, None]
    )
    lo = jnp.argmax(meets, axis=2).astype(jnp.int32)
    n = jnp.sum(meets, axis=2).astype(jnp.int32)
    word = jnp.broadcast_to((kinds.reshape(tokens, 1) == 0).astype(F32), (tokens, 128))
    lane = lax.broadcasted_iota(jnp.int32, (tokens, 128), 1)
    own = segments.reshape(tokens, 1) == lane
    mk = own.astype(BF)
    mq = jnp.where(jnp.logical_and(lane < 4, jnp.logical_not(own)), -FAR, 0.0).astype(BF)
    return lo, n, word, mq, mk


def gathered_vectors(sizes, everyone):
    spans, parts, at, start = [], [], 0, 0
    for size in sizes:
        parts.append(everyone[:, at : at + size].reshape(1, -1))
        spans.append((start, size * everyone.shape[0]))
        at += size
        start += size * everyone.shape[0]
    return jnp.concatenate(parts, 1).astype(F32), spans


def tie(value, deps):
    return lax.optimization_barrier((value, *deps))[0] if deps else value


def by_dp(bit):
    return lambda v: lax.ppermute(v, DP, [(i, i ^ bit) for i in range(16)])


def over_y(v):
    return lax.ppermute(v, FSDP, [(0, 1), (1, 0)])


over_core, over_x, over_z, over_far_z = (by_dp(1 << k) for k in range(4))


class NearWeights:
    def __init__(self, weights, vectors, pos, width, hidden):
        self.weights, self.pos, self.width = weights, pos, width
        groups = width // GROUP
        self.shard, self.part = width // 2, width // 8
        self.d_shard, self.d_part = hidden // 2, hidden // 8
        self.columns = 2 * width
        o_rows, i_rows, d_rows = self.part // 2, self.part, self.d_part // 2
        self.rows = o_rows, i_rows, d_rows

        def chunk(size, more=0):
            return lambda pos: (2 * pos[2] + pos[1]) * size + more

        def group_loads(group, to, row):
            return [
                (source, ((chunk(self.part), self.part), (column, GROUP)), ((row, self.part), (k * GROUP, GROUP)), to)
                for k, (source, column) in enumerate(group_columns(group, width))
            ]

        first = call_pack(pos, weights[:2], [(self.part, self.columns)], group_loads(0, 0, 0))[0]
        loads = []
        for group in range(1, groups):
            loads += group_loads(group, 0, (group - 1) * self.part)
        for side in range(2):
            at = (side * width, width)
            loads.append((2, ((chunk(self.part, side * o_rows), o_rows), (0, width)), ((0, o_rows), at), 1))
            loads.append(
                (
                    3,
                    ((chunk(self.part), i_rows), (side * self.columns, self.columns)),
                    ((o_rows + side * i_rows, i_rows), (0, self.columns)),
                    1,
                )
            )
            loads.append((4, ((chunk(self.d_part, side * d_rows), d_rows), (0, width)), ((0, d_rows), at), 2))
        shapes = [(groups - 1) * self.part, o_rows + 2 * i_rows, d_rows]
        self.from_y = [over_y(first)]
        packs = call_pack(tie(pos, (first,)), weights, [(rows, self.columns) for rows in shapes], loads)
        other = over_y(tie(vectors, (first,)))
        self.from_y += [over_y(v) for v in packs]
        vec = jnp.where(pos[0] == 0, jnp.stack([vectors, other]), jnp.stack([other, vectors]))
        self.vec = vec.astype(F32)
        self.arrived = [None] * 4

    def spread(self, k, before_x=(), before_core=()):
        v = tie(self.from_y[k], before_x)
        from_x = over_x(v)
        self.arrived[k] = [v, from_x, over_core(v), over_core(tie(from_x, before_core))]

    def others(self, size, more=0):
        other = lambda turn: lambda pos: (4 * (1 - pos[0]) + ((2 * pos[2] + pos[1]) ^ turn)) * size + more
        return [other(turn) for turn in (0, 2, 1, 3)]

    def own(self, size):
        return lambda pos: pos[0] * size

    def group(self, group):
        width, part = self.width, self.part
        loads = [
            (source, ((0, self.shard), (column, GROUP)), ((self.own(self.shard), self.shard), (k * GROUP, GROUP)))
            for k, (source, column) in enumerate(group_columns(group, width))
        ]
        row = 0 if group == 0 else (group - 1) * part
        for k, place in enumerate(self.others(part)):
            at = (0, self.columns)
            loads.append((2 + k, ((row, part), at), ((place, part), at)))
        return self.weights[:2] + self.arrived[min(group, 1)], loads

    def rest(self):
        width, columns = self.width, self.columns
        o_rows, i_rows, d_rows = self.rows
        whole_o, whole_i = (0, width), (0, 2 * columns)
        loads = [
            [(0, ((0, self.shard), whole_o), ((self.own(self.shard), self.shard), whole_o))],
            [(1, ((0, self.shard), whole_i), ((self.own(self.shard), self.shard), whole_i))],
            [(2, ((0, self.d_shard), whole_o), ((self.own(self.d_shard), self.d_shard), whole_o))],
        ]
        for side in range(2):
            at = (side * width, width)
            for k, place in enumerate(self.others(self.part, side * o_rows)):
                loads[0].append((3 + k, ((0, o_rows), at), ((place, o_rows), whole_o)))
            for k, place in enumerate(self.others(self.part)):
                from_rows = (o_rows + side * i_rows, i_rows)
                to = (side * columns, columns)
                loads[1].append((3 + k, (from_rows, (0, columns)), ((place, i_rows), to)))
            for k, place in enumerate(self.others(self.d_part, side * d_rows)):
                loads[2].append((7 + k, ((0, d_rows), at), ((place, d_rows), whole_o)))
        return self.weights[2:] + self.arrived[2] + self.arrived[3], loads


class FarWeights:
    def __init__(self, weights, vectors, sizes, width, hidden):
        self.weights = [lax.all_gather(v, FSDP, axis=0, tiled=True) for v in weights]
        self.vec, self.spans = gathered_vectors(sizes, lax.all_gather(vectors, FSDP))
        self.width = width

    def group(self, group):
        rows = (0, self.width)
        loads = [
            (source, (rows, (column, GROUP)), (rows, (k * GROUP, GROUP)))
            for k, (source, column) in enumerate(group_columns(group, self.width))
        ]
        return self.weights[:2], loads

    def rest(self):
        loads = []
        for k, v in enumerate(self.weights[2:]):
            spec = tuple((0, size) for size in v.shape)
            loads.append([(k, spec, spec)])
        return self.weights[2:], loads


def group_columns(group, width):
    blocks = [(0, part * width + group * GROUP) for part in range(4)]
    return blocks + [(1, part * width + group * GROUP) for part in range(2)]


def body(mesh_shape, hidden_in, segments, kinds, *rest):
    weights = [rest[i] for i in (0, 2, 4, 8, 10)]
    vectors = [rest[i] for i in (1, 3, 5, 6, 7, 9, 11, 12, 13)]
    near = mesh_shape[DP] == 16 and mesh_shape[FSDP] == 2
    seqs, length, width = hidden_in.shape
    tokens = seqs * length
    groups = width // GROUP
    x = hidden_in.reshape(tokens, width)
    g = rest[14].reshape(tokens, width)
    fsdp = mesh_shape[FSDP]
    hidden = weights[4].shape[0] * fsdp
    y, place = lax.axis_index(FSDP), lax.axis_index(DP)
    sizes = [v.shape[0] for v in vectors]
    total, start, parts, spans = sum(sizes), 0, [], []
    for v, size in zip(vectors, sizes):
        parts.append(lax.pad(v, jnp.zeros((), BF), [(start, total - start - size, 0)]))
        spans.append((start, size))
        start += size
    vector_shard = sum(parts[1:], parts[0])
    if near:
        bits = jnp.array([0, 1, 2, 4], jnp.int32)
        pos = jnp.stack([y, place & 1, (place >> 1) & 1]).astype(jnp.int32)
        source = NearWeights(weights, vector_shard, pos, width, hidden)
        source.spread(0)
    else:
        pos = jnp.ones((3,), jnp.int32)
        source = FarWeights(weights, vector_shard, sizes, width, hidden)
        spans = source.spans
    vec = source.vec
    lo, n, word, mq, mk = document_facts(segments, kinds)
    kept = []
    for group in range(groups):
        deps = tuple(k[3] for k in kept[-1:])
        if near and group == 0:
            deps = (source.from_y[1],)
        if near and group == 1:
            source.spread(1, (), (kept[0][3],))
        refs, loads = source.group(group)
        kept.append(
            call_qkv_attention(
                group, lo, n, pos, tie(x, deps), vec, spans, word, mq, mk, refs, loads
            )
        )
    if near:
        source.spread(2, (kept[0][3],), (kept[1][3],))
        source.spread(3, (kept[0][3],), (kept[2][3],))
    refs, loads = source.rest()
    context, hat, inverse, first_low, act, slope = call_output_norm_inner(
        pos, [k[3] for k in kept], x, vec, spans, refs, loads, hidden
    )
    output, summed, gb, small_ffn = call_down_norm(pos, act, hat, g, vec, spans, refs, loads)

    made, sent, partial_sums, results = {}, {}, {}, {}

    def run(kernel, deps):
        kind, k = kernel
        if kind == DOWN:
            made[kind] = call_down_grad(pos, tie(act, deps), gb)
            return made[kind][:1]
        if kind == BACK:
            results[kind] = call_inner_back(
                pos, tie(gb, deps), slope, summed, hat, inverse, vec, spans, refs, loads
            )
            return results[kind][:1]
        gi, gx, ga, gc, small_attn = results[BACK]
        if kind == INNER:
            made[kind] = call_projection_grad(
                pos, tie(first_low, deps), gi, (context, ga, small_ffn, small_attn)
            )
            return made[kind][:1]
        if kind == ATTENTION:
            partial_sums[k] = call_attention_back(k, lo, n, kept[k], tie(gc, deps), word, mq, mk)
            return (partial_sums[k],)
        if kind == PROJECTION:
            made[k] = call_projection_grad(pos, tie(x, deps), partial_sums[k])
            return made[k][:1]
        group_refs, group_loads = source.group(k)
        results[TOKEN] = call_token_grad(
            pos, partial_sums[k], tie(results.get(TOKEN, gx), deps), group_refs, group_loads,
            BF if k == groups - 1 else F32,
        )
        return (results[TOKEN],)

    order = [(DOWN, 0), (BACK, 0), (INNER, 0)]
    for k in range(groups):
        order += [(ATTENTION, k), (PROJECTION, k)]
    order += [(TOKEN, k) for k in range(groups)]

    def halves(k, v):
        if k == DOWN:
            h = v.shape[0] // 2
            return v[:h], v[h:]
        h = v.shape[1] // 2
        return v[:, :h], v[:, h:]

    def advance(k, step, deps):
        if step == 0:
            sent[k] = (over_core(made[k][0]), made[k][1])
            return ()
        come, mine = sent[k]
        come = tie(come, deps)
        if step == 1:
            out = [plus(mine[i], come[i]) for i in range(2)]
            sent[k] = (over_y(out[0]), out[1])
        elif step == 2:
            out = [plus(a, b) for a, b in zip(halves(k, mine), halves(k, come))]
            sent[k] = (over_x(out[0]), out[1])
        elif step in (3, 4):
            out = [plus(mine, come)]
            sent[k] = ((over_z if step == 3 else over_far_z)(out[0]), out[0])
        elif step == 5:
            out = [plus(mine, come)]
            sent[k] = (over_x(out[0]), [out[0], over_core(out[0])])
        else:
            out = [come]
            sent[k] = [mine[0], come, mine[1], over_core(come)]
        return tuple(out)

    def finished(k):
        if k == DOWN:
            results[k] = small_call(join_down, "join_down", pos, sent[k], [((hidden // 2, width), F32)])[0]
            return (results[k],)
        shard = width // 2
        results[k] = small_call(
            join_inner, "join_inner", pos, sent[k],
            [((shard, hidden), F32), ((shard, width), F32), ((EXTRA, hidden), F32)],
        )
        return tuple(results[k][:1])

    if near:
        plan = {}
        for k, steps in STEPS.items():
            for step, after in enumerate(steps):
                plan.setdefault(after, []).append((step, k))
        deps = ()
        for i in range(max(plan) + 1):
            done = ()
            if i < len(order):
                done = run(order[i], deps)
            deps = done
            for step, k in sorted(plan.get(i, []), key=lambda item: -item[0]):
                deps = deps + (finished(k) if step == 7 else advance(k, step, done))
        grad_inner, grad_output, extra = results[INNER]
        shard = width // 2
        grad_query, grad_key_value, small, _ = small_call(
            partial(join_groups, groups), "join_groups", pos,
            [extra] + [v for k in range(groups) for v in sent[k]],
            [
                ((shard, 4 * width), F32),
                ((shard, 2 * width), F32),
                ((1, total), F32),
                ((groups, EXTRA, 6 * GROUP), F32),
            ],
        )
        small = small.reshape(total)
        shares = [small[start : start + size] for start, size in spans]
        grad_down = results[DOWN]
    else:
        for kernel in order:
            run(kernel, ())

        def flat(v):
            return v.reshape(v.shape[0], -1).astype(F32)

        def far(v):
            return lax.psum(lax.psum_scatter(v, FSDP, scatter_dimension=0, tiled=True), DP)

        def main_and_extra(k, rows):
            both = jnp.stack(made[k], 2)
            main = both[:, :rows].reshape(2 * rows, 2, -1)
            more = both[1, rows : rows + EXTRA]
            return flat(far(main)), flat(lax.psum(more, (DP, FSDP)))

        rows = width // 2
        grad_inner, wide = main_and_extra(INNER, rows)
        grad_down = flat(far(jnp.stack(made[DOWN], 2).reshape(hidden, 2, -1)))
        out = jnp.stack(made[INNER], 0)[:, :, rows + EXTRA :]
        eighth = out.shape[2]
        out = out.reshape(2, 2, eighth, 4, width // 2).transpose(1, 3, 2, 0, 4)
        grad_output = flat(far(out.reshape(width, 2, -1)))
        by_group, late = zip(*[main_and_extra(k, rows) for k in range(groups)])
        late = [e[0] for e in late]
        early = [wide[1 + i, k * width : (k + 1) * width] for i in range(2) for k in range(4)]
        gain_ffn, bias_ffn, b_down, gain_attn, bias_attn, b_output = early[:6]
        query = jnp.concatenate([e[k * GROUP : (k + 1) * GROUP] for k in range(4) for e in late])
        value = jnp.concatenate([e[5 * GROUP :] for e in late])
        order = (query, value, b_output, gain_attn, bias_attn, wide[0], b_down, gain_ffn, bias_ffn)
        shares = [lax.dynamic_slice_in_dim(v, y * size, size, 0) for v, size in zip(order, sizes)]
        grad_query = jnp.concatenate(
            [m[:, k * GROUP : (k + 1) * GROUP] for k in range(4) for m in by_group], 1
        )
        grad_key_value = jnp.concatenate(
            [m[:, k * GROUP : (k + 1) * GROUP] for k in range(4, 6) for m in by_group], 1
        )
    return (
        output.reshape(seqs, length, width),
        results[TOKEN].reshape(seqs, length, width),
        grad_query,
        shares[B_QUERY],
        grad_key_value,
        shares[B_VALUE],
        grad_output,
        shares[B_OUTPUT],
        shares[GAIN_ATTN],
        shares[BIAS_ATTN],
        grad_inner,
        shares[B_INNER],
        grad_down,
        shares[B_DOWN],
        shares[GAIN_FFN],
        shares[BIAS_FFN],
    )


DOWN, BACK, INNER, ATTENTION, PROJECTION, TOKEN = range(-6, 0)
STEPS = {
    DOWN: (0, 1, 3, 5, 6, 8, 9, 10),
    INNER: (2, 3, 6, 7, 8, 10, 11, 12),
    0: (4, 5, 8, 9, 10, 11, 12),
    1: (6, 7, 9, 10, 11, 12, 13),
    2: (8, 9, 10, 11, 12, 13, 14),
}
BACK_ROWS = 640


def solution(mesh):
    split = P((DP, FSDP), None, None)
    tokens = P((DP, FSDP), None)
    matrix, line = P(FSDP, None), P(FSDP)
    weights = (matrix, line, matrix, line, matrix, line, line, line, matrix, line, matrix, line, line, line)
    return jax.shard_map(
        partial(body, dict(mesh.shape)),
        mesh=mesh,
        in_specs=(split, tokens, tokens) + weights + (split,),
        out_specs=(split, split) + weights,
        check_vma=False,
    )
```

time: 1230 us -> 470 us (0.38)
  matrix products: 628 us -> 0 us
  Pallas kernels: 0 us -> 281 us
  waiting for transfers between devices: 295 us -> 102 us
  blocking collectives: 110 us -> 0 us
  local copies, waits for them, and re-layouts: 110 us -> 12.8 us
  starting transfers between devices: 0.82 us -> 53.5 us
  other arithmetic: 53.7 us -> 13.7 us
  between operations: 17.1 us -> 1.78 us
    dot_general x294 -> x0, matrix products: 628 us -> none  [the longest x130 234 us: times_transpose(): lax.dot_general(left, right, (((1,), (1,)), ((), ())), preferred_element_...]
    pallas_call x0 -> x22, Pallas kernels: none -> 281 us  [the longest x3 51.9 us: call_qkv_attention(): pl.pallas_call(partial(qkv_attention, loads, spans, group, len(refs)), ou...]
    reduce_scatter x3 -> x0, waiting for transfers between devices: 146 us -> none  [the longest x1 63 us: body(): lax.psum_scatter(totals[10].astype(jnp.bfloat16), 'fsdp', scatter_dimensi...]
    ppermute x0 -> x57, waiting for transfers between devices: none -> 102 us  [the longest x47 77.5 us: by_dp(): return lambda v: lax.ppermute(v, DP, [(i, i ^ bit) for i in range(16)])]
    psum x1 -> x0, waiting for transfers between devices: 83.1 us -> none  [body(): lax.psum(shares[0].astype(jnp.bfloat16), 'dp').astype(jnp.float32)]
    psum x1 -> x0, blocking collectives: 63.2 us -> none  [body(): lax.psum(shares[1].astype(jnp.bfloat16), 'dp').astype(jnp.float32)]
    ppermute x0 -> x57, starting transfers between devices: none -> 53.5 us  [the longest x47 39.1 us: by_dp(): return lambda v: lax.ppermute(v, DP, [(i, i ^ bit) for i in range(16)])]
    unnamed x265 -> x106, local copies, waits for them, and re-layouts: 60.6 us -> 7.35 us
  transfers between devices with their start and end apart: 11 -> 57, of which waited for: 6 -> 16; matrix products, arithmetic and copies ran while one was open for 26% -> 3% of each run, Pallas kernels for 0% -> 42%
where the time goes in v1:
time: 470 us; the launch traced here: 465 us
  Pallas kernels  281 us (60%)
  waiting for transfers between devices  102 us (22%)
  starting transfers between devices  53.5 us (11%)
  other arithmetic  13.7 us (3%)
  local copies, waits for them, and re-layouts  12.8 us (3%)
    ppermute x47, waiting for transfers between devices, by_dp(): return lambda v: lax.ppermute(v, DP, [(i, i ^ bit) for i in range(16)])  77.5 us
    pallas_call x3, Pallas kernels, call_qkv_attention(): pl.pallas_call(partial(qkv_attention, loads, spans, group, len(refs)), ou...  51.9 us
    pallas_call x3, Pallas kernels, call_attention_back(): pl.pallas_call(attention_back, out_shape=shaped((tokens, 6 * GROUP), BF),...  42 us
    pallas_call x1, Pallas kernels, call_inner_back(): pl.pallas_call(partial(inner_back, loads, spans, len(refs)), out_shape=[s...  41.4 us
    pallas_call x4, Pallas kernels, call_projection_grad(): pl.pallas_call(inner_output_grad if more else projection_grad, out_shape=...  41.2 us
    ppermute x47, starting transfers between devices, by_dp(): return lambda v: lax.ppermute(v, DP, [(i, i ^ bit) for i in range(16)])  39.1 us
    pallas_call x3, Pallas kernels, call_token_grad(): pl.pallas_call(partial(token_grad, loads, len(refs)), out_shape=shaped((t...  28.8 us
    ppermute x10, waiting for transfers between devices, over_y(): return lax.ppermute(v, FSDP, [(0, 1), (1, 0)])  24.7 us
  transfers between devices with their start and end apart: 57, of which 16 were waited for; matrix products, arithmetic and copies ran while one was open for 3% of the time, Pallas kernels for 42%

profile of v1, /device:TPU:0, one launch (start us, length us, event | category | flops | bytes accessed | tf_op | source)
XLA Modules:
  0.0 465.3 jit_solution(17318703204427451812)
XLA Ops:
  31.7 17.2 %qkv_attention.3 = (bf16[1280,512]{1,0:T(8,128)(2,1)}, bf16[1280,512]{1,0:T(8,128)(2,1)}, bf16[1280,256]{1,0:T(8,128)(2,1)}, bf16[1280,256]{1,0:T(8,128)(2,1)}, f32[2,5,8,128]{3,2,1,0:T(8,128)}) custom-call(s32[2,5]{1,0:T(2,128)} %copy.36.lo_ref, s32[2,5]{1,0:T(2,128)} %copy.37.n_ref, s32[3]{0:T(128)} %pad_add_fusion.1.pos_ref.at_ref, ...), custom_call_target="tpu_custom_call" | custom-call | flops 6000000000 | bytes 12582912 | tf_op jit(solution)/shard_map/qkv_attention/pallas_call | solution.py:210
  59.2 17.2 %qkv_attention.4 = (bf16[1280,512]{1,0:T(8,128)(2,1)}, bf16[1280,512]{1,0:T(8,128)(2,1)}, bf16[1280,256]{1,0:T(8,128)(2,1)}, bf16[1280,256]{1,0:T(8,128)(2,1)}, f32[2,5,8,128]{3,2,1,0:T(8,128)}) custom-call(s32[2,5]{1,0:T(2,128)} %copy.36.lo_ref, s32[2,5]{1,0:T(2,128)} %copy.37.n_ref, s32[3]{0:T(128)} %pad_add_fusion.1.pos_ref.at_ref, ...), custom_call_target="tpu_custom_call" | custom-call | flops 6000000000 | bytes 12582912 | tf_op jit(solution)/shard_map/qkv_attention/pallas_call | solution.py:210
  77.3 17.5 %qkv_attention.5 = (bf16[1280,512]{1,0:T(8,128)(2,1)}, bf16[1280,512]{1,0:T(8,128)(2,1)}, bf16[1280,256]{1,0:T(8,128)(2,1)}, bf16[1280,256]{1,0:T(8,128)(2,1)}, f32[2,5,8,128]{3,2,1,0:T(8,128)}) custom-call(s32[2,5]{1,0:T(2,128)} %copy.36.lo_ref, s32[2,5]{1,0:T(2,128)} %copy.37.n_ref, s32[3]{0:T(128)} %pad_add_fusion.1.pos_ref.at_ref, ...), custom_call_target="tpu_custom_call" | custom-call | flops 6000000000 | bytes 12582912 | tf_op jit(solution)/shard_map/qkv_attention/pallas_call | solution.py:210
  99.0 23.1 %output_norm_inner.1 = (bf16[1280,768]{1,0:T(8,128)(2,1)}, f32[1280,768]{1,0:T(8,128)}, f32[1280,128]{1,0:T(8,128)}, bf16[1280,768]{1,0:T(8,128)(2,1)}, bf16[128...) custom-call(s32[3]{0:T(128)} %pad_add_fusion.1.pos_ref.at_ref, bf16[1280,768]{1,0:T(8,128)(2,1)} %bitcast.39, ...), custom_call_target="tpu_custom_call" | custom-call | flops 7549747200 | bytes 31457280 | tf_op jit(solution)/shard_map/output_norm_inner/pallas_call | solution.py:408
  122.1 18.9 %down_norm.1 = (bf16[1280,768]{1,0:T(8,128)(2,1)}, f32[1280,768]{1,0:T(8,128)}, bf16[1280,768]{1,0:T(8,128)(2,1)}, f32[8,768]{1,0:T(8,128)}) custom-call(s32[3]{0:T(128)} %pad_add_fusion.1.pos_ref.at_ref, bf16[1280,3072]{1,0:T(8,128)(2,1)} %get-tuple-element.128.act_ref.left_ref, f32[1280,768]{1,0:T(8,128)} %get-tuple-element.129.hat_ref, ...), custom_call_target="tpu_custom_call" | custom-call | flops 6039797760 | bytes 20971520 | tf_op jit(solution)/shard_map/down_norm/pallas_call | solution.py:475
  141.1 12.8 %down_grad.1 = (bf16[2,1536,384]{2,1,0:T(8,128)(2,1)}, bf16[2,1536,384]{2,1,0:T(8,128)(2,1)}) custom-call(s32[3]{0:T(128)} %pad_add_fusion.1.pos_ref.at_ref, bf16[1280,3072]{1,0:T(8,128)(2,1)} %get-tuple-element.128.act_ref.left_ref, bf16[1280,768]{1,0:T(8,128)(2,1)} %get-tuple-element.133.right_ref.gb_ref), custom_call_target="tpu_custom_call" | custom-call | flops 12999999488 | bytes 12582912 | tf_op jit(solution)/shard_map/down_grad/pallas_call | solution.py:616
  154.2 41.4 %inner_back.1 = (bf16[1280,3072]{1,0:T(8,128)(2,1)}, f32[1280,768]{1,0:T(8,128)}, bf16[1280,768]{1,0:T(8,128)(2,1)}, bf16[1280,768]{1,0:T(8,128)(2,1)}, f32[8,768]{1,0:T(8,128)}) custom-call(s32[3]{0:T(128)} %pad_add_fusion.1.pos_ref.at_ref, bf16[1280,768]{1,0:T(8,128)(2,1)} %get-tuple-element.133.right_ref.gb_ref, ...), custom_call_target="tpu_custom_call" | custom-call | flops 13589544960 | bytes 31457280 | tf_op jit(solution)/shard_map/inner_back/pallas_call | solution.py:555
  196.2 15.4 %projection_grad.4 = (bf16[2,496,1536]{2,1,0:T(8,128)(2,1)}, bf16[2,496,1536]{2,1,0:T(8,128)(2,1)}) custom-call(s32[3]{0:T(128)} %pad_add_fusion.1.pos_ref.at_ref, bf16[1280,768]{1,0:T(8,128)(2,1)} %get-tuple-element.152.left_ref, bf16[1280,3072]{1,0:T(8,128)(2,1)} %get-tuple-element.149.right_ref, bf16[1280,768]{1,0:T(8,128)(2,1)} %get-tuple-element.153.context_ref, ...), custom_call_target="tpu_custom_call" | custom-call | flops 17999998976 | bytes 12582912 | tf_op jit(solution)/shard_map/projection_grad/pallas_call | solution.py:688
  214.1 13.9 %attention_back.3.right_ref.part_ref = bf16[1280,1536]{1,0:T(8,128)(2,1)} custom-call(s32[2,5]{1,0:T(2,128)} %copy.36.lo_ref, s32[2,5]{1,0:T(2,128)} %copy.37.n_ref, bf16[1280,512]{1,0:T(8,128)(2,1)} %get-tuple-element.145.qd_ref, bf16[1280,512]{1,0:T(8,128)(2,1)} %get-tuple-element.146.kd_ref, bf16[1280,256]{1,0:T(8,128)(2,1)} %get-tuple-element.147.v_ref, ...), custom_call_target="tpu_custom_call" | custom-call | flops 6000000000 | bytes 12582912 | tf_op jit(solution)/shard_map/attention_back/pallas_call | solution.py:336
  228.0 12.6 %collective-permute-done.18 = bf16[1536,384]{1,0:T(8,128)(2,1)S(1)} collective-permute-done((bf16[1536,384]{1,0:T(8,128)(2,1)S(1)}, bf16[1536,384]{1,0:T(8,128)(2,1)S(1)}, u32[]{:S(2)}, u32[]{:S(2)}) %collective-permute-start.18) | collective-permute-done | bytes 1179680 | tf_op jit(solution)/shard_map/ppermute | solution.py:884
  243.5 8.7 %projection_grad.5 = (bf16[2,400,768]{2,1,0:T(8,128)(2,1)}, bf16[2,400,768]{2,1,0:T(8,128)(2,1)}) custom-call(s32[3]{0:T(128)} %pad_add_fusion.1.pos_ref.at_ref, bf16[1280,768]{1,0:T(8,128)(2,1)} %bitcast.40, bf16[1280,1536]{1,0:T(8,128)(2,1)} %attention_back.3.right_ref.part_ref), custom_call_target="tpu_custom_call" | custom-call | flops 8999999488 | bytes 12582912 | tf_op jit(solution)/shard_map/projection_grad/pallas_call | solution.py:688
  255.0 14.2 %attention_back.4.right_ref.part_ref = bf16[1280,1536]{1,0:T(8,128)(2,1)} custom-call(s32[2,5]{1,0:T(2,128)} %copy.36.lo_ref, s32[2,5]{1,0:T(2,128)} %copy.37.n_ref, bf16[1280,512]{1,0:T(8,128)(2,1)} %get-tuple-element.142.qd_ref, bf16[1280,512]{1,0:T(8,128)(2,1)} %get-tuple-element.143.kd_ref, bf16[1280,256]{1,0:T(8,128)(2,1)} %get-tuple-element.144.v_ref, ...), custom_call_target="tpu_custom_call" | custom-call | flops 6000000000 | bytes 12582912 | tf_op jit(solution)/shard_map/attention_back/pallas_call | solution.py:336
  275.8 8.6 %projection_grad.6 = (bf16[2,400,768]{2,1,0:T(8,128)(2,1)}, bf16[2,400,768]{2,1,0:T(8,128)(2,1)}) custom-call(s32[3]{0:T(128)} %pad_add_fusion.1.pos_ref.at_ref, bf16[1280,768]{1,0:T(8,128)(2,1)} %bitcast.41, bf16[1280,1536]{1,0:T(8,128)(2,1)} %attention_back.4.right_ref.part_ref), custom_call_target="tpu_custom_call" | custom-call | flops 8999999488 | bytes 12582912 | tf_op jit(solution)/shard_map/projection_grad/pallas_call | solution.py:688
  294.9 14.0 %attention_back.5.right_ref.part_ref = bf16[1280,1536]{1,0:T(8,128)(2,1)} custom-call(s32[2,5]{1,0:T(2,128)} %copy.36.lo_ref, s32[2,5]{1,0:T(2,128)} %copy.37.n_ref, bf16[1280,512]{1,0:T(8,128)(2,1)} %get-tuple-element.138.qd_ref, bf16[1280,512]{1,0:T(8,128)(2,1)} %get-tuple-element.139.kd_ref, bf16[1280,256]{1,0:T(8,128)(2,1)} %get-tuple-element.140.v_ref, ...), custom_call_target="tpu_custom_call" | custom-call | flops 6000000000 | bytes 12582912 | tf_op jit(solution)/shard_map/attention_back/pallas_call | solution.py:336
  312.5 8.6 %projection_grad.7 = (bf16[2,400,768]{2,1,0:T(8,128)(2,1)}, bf16[2,400,768]{2,1,0:T(8,128)(2,1)}) custom-call(s32[3]{0:T(128)} %pad_add_fusion.1.pos_ref.at_ref, bf16[1280,768]{1,0:T(8,128)(2,1)} %bitcast.42, bf16[1280,1536]{1,0:T(8,128)(2,1)} %attention_back.5.right_ref.part_ref), custom_call_target="tpu_custom_call" | custom-call | flops 8999999488 | bytes 12582912 | tf_op jit(solution)/shard_map/projection_grad/pallas_call | solution.py:688
  323.1 12.5 %collective-permute-done.27 = bf16[496,768]{1,0:T(8,128)(2,1)S(1)} collective-permute-done((bf16[496,768]{1,0:T(8,128)(2,1)S(1)}, bf16[496,768]{1,0:T(8,128)(2,1)S(1)}, u32[]{:S(2)}, u32[]{:S(2)}) %collective-permute-start.27) | collective-permute-done | bytes 761888 | tf_op jit(solution)/shard_map/ppermute | solution.py:880
  336.7 9.7 %token_grad.3.sum_ref = f32[1280,768]{1,0:T(8,128)} custom-call(s32[3]{0:T(128)} %pad_add_fusion.1.pos_ref.at_ref, f32[1280,768]{1,0:T(8,128)} %get-tuple-element.184.sum_ref, bf16[1280,1536]{1,0:T(8,128)(2,1)} %attention_back.3.right_ref.part_ref, bf16[384,3072]{1,0:T(8,128)(2,1)} %rest_0_.19, bf16[384,1536]{1,0:T(8,128)(2,1)} %rest_1_.19, ...), custom_call_target="tpu_custom_call" | custom-call | flops 8000000000 | bytes 12582912 | tf_op jit(solution)/shard_map/token_grad/pallas_call | solution.py:828
  357.6 9.8 %token_grad.4.sum_ref = f32[1280,768]{1,0:T(8,128)} custom-call(s32[3]{0:T(128)} %pad_add_fusion.1.pos_ref.at_ref, f32[1280,768]{1,0:T(8,128)} %token_grad.3.sum_ref, bf16[1280,1536]{1,0:T(8,128)(2,1)} %attention_back.4.right_ref.part_ref, bf16[384,3072]{1,0:T(8,128)(2,1)} %rest_0_.19, bf16[384,1536]{1,0:T(8,128)(2,1)} %rest_1_.19, ...), custom_call_target="tpu_custom_call" | custom-call | flops 8000000000 | bytes 12582912 | tf_op jit(solution)/shard_map/token_grad/pallas_call | solution.py:828
  374.8 15.4 %collective-permute-done.35 = bf16[496,768]{1,0:T(8,128)(2,1)S(1)} collective-permute-done((bf16[496,768]{1,0:T(8,128)(2,1)S(1)}, bf16[496,768]{1,0:T(8,128)(2,1)S(1)}, u32[]{:S(2)}, u32[]{:S(2)}) %collective-permute-start.35) | collective-permute-done | bytes 761888 | tf_op jit(solution)/shard_map/ppermute | solution.py:880
  391.9 9.3 %token_grad.5 = bf16[1280,768]{1,0:T(8,128)(2,1)} custom-call(s32[3]{0:T(128)} %pad_add_fusion.1.pos_ref.at_ref, f32[1280,768]{1,0:T(8,128)} %token_grad.4.sum_ref, bf16[1280,1536]{1,0:T(8,128)(2,1)} %attention_back.5.right_ref.part_ref, bf16[384,3072]{1,0:T(8,128)(2,1)} %rest_0_.19, bf16[384,1536]{1,0:T(8,128)(2,1)} %rest_1_.19, ...), custom_call_target="tpu_custom_call" | custom-call | flops 8000000000 | bytes 12582912 | tf_op jit(solution)/shard_map/token_grad/pallas_call | solution.py:828
  404.9 7.3 %collective-permute-done.52 = bf16[400,384]{1,0:T(8,128)(2,1)S(1)} collective-permute-done((bf16[400,384]{1,0:T(8,128)(2,1)S(1)}, bf16[400,384]{1,0:T(8,128)(2,1)S(1)}, u32[]{:S(2)}, u32[]{:S(2)}) %collective-permute-start.52) | collective-permute-done | bytes 307232 | tf_op jit(solution)/shard_map/ppermute | solution.py:880
  414.3 6.4 %collective-permute-done.39.rest_1_ = bf16[496,768]{1,0:T(8,128)(2,1)S(1)} collective-permute-done((bf16[496,768]{1,0:T(8,128)(2,1)S(1)}, bf16[496,768]{1,0:T(8,128)(2,1)S(1)}, u32[]{:S(2)}, u32[]{:S(2)}) %collective-permute-start.39) | collective-permute-done | bytes 761888 | tf_op jit(solution)/shard_map/ppermute | solution.py:880
  421.6 7.1 %collective-permute-done.47 = bf16[400,384]{1,0:T(8,128)(2,1)S(1)} collective-permute-done((bf16[400,384]{1,0:T(8,128)(2,1)S(1)}, bf16[400,384]{1,0:T(8,128)(2,1)S(1)}, u32[]{:S(2)}, u32[]{:S(2)}) %collective-permute-start.47) | collective-permute-done | bytes 307232 | tf_op jit(solution)/shard_map/ppermute | solution.py:880
  437.6 7.5 %collective-permute-done.48.rest_6_ = bf16[400,384]{1,0:T(8,128)(2,1)S(1)} collective-permute-done((bf16[400,384]{1,0:T(8,128)(2,1)S(1)}, bf16[400,384]{1,0:T(8,128)(2,1)S(1)}, u32[]{:S(2)}, u32[]{:S(2)}) %collective-permute-start.48) | collective-permute-done | bytes 307232 | tf_op jit(solution)/shard_map/ppermute | solution.py:880
  (264 shorter events, 134.7 us)
Async XLA Ops:
  12.8 44.3 %collective-permute-start.13 = (bf16[192,1536]{1,0:T(8,128)(2,1)}, bf16[192,1536]{1,0:T(8,128)(2,1)S(1)}, u32[]{:S(2)}, u32[]{:S(2)}) collective-permute-start(bf16[192,1536]{1,0:T(8,128)(2,1)} %get-tuple-element.125), channel_id=1, source_target_pairs={{0,1},{1,0},{2,3},{3,2},{4,5},{5,4},{6,7},{7,6},{8,9},{9,8},{10,11... | collective-permute-start | bytes 1769480 | tf_op jit(solution)/shard_map/ppermute | solution.py:884
  12.9 42.5 %collective-permute-start.9 = (bf16[240,1536]{1,0:T(8,128)(2,1)}, bf16[240,1536]{1,0:T(8,128)(2,1)S(1)}, u32[]{:S(2)}, u32[]{:S(2)}) collective-permute-start(bf16[240,1536]{1,0:T(8,128)(2,1)} %get-tuple-element.122), channel_id=1, source_target_pairs={{0,1},{1,0},{2,3},{3,2},{4,5},{5,4},{6,7},{7,6},{8,9},{9,8},{10,11... | collective-permute-start | bytes 2211848 | tf_op jit(solution)/shard_map/ppermute | solution.py:884
  30.5 27.0 %collective-permute-start.7 = (bf16[192,1536]{1,0:T(8,128)(2,1)S(1)}, bf16[192,1536]{1,0:T(8,128)(2,1)S(1)}, u32[]{:S(2)}, u32[]{:S(2)}) collective-permute-start(bf16[192,1536]{1,0:T(8,128)(2,1)S(1)} %collective-permute-done.1.rest_2_), channel_id=1, source_target_pairs={{0,2},{2,0},{4,6},{6,4},{8,10},{10,8},{12,14},{14,12},{16,18},{18,... | collective-permute-start | bytes 1769480 | tf_op jit(solution)/shard_map/ppermute | solution.py:880
  57.1 38.5 %collective-permute-start.15 = (bf16[192,1536]{1,0:T(8,128)(2,1)S(1)}, bf16[192,1536]{1,0:T(8,128)(2,1)S(1)}, u32[]{:S(2)}, u32[]{:S(2)}) collective-permute-start(bf16[192,1536]{1,0:T(8,128)(2,1)S(1)} %collective-permute-done.13.rest_10_.rest_7_), channel_id=1, source_target_pairs={{0,2},{2,0},{4,6},{6,4},{8,10},{10,8},{12,14},{14,12},{16,18},{18,... | collective-permute-start | bytes 1769480 | tf_op jit(solution)/shard_map/ppermute | solution.py:880
  57.1 37.7 %collective-permute-start.14 = (bf16[192,1536]{1,0:T(8,128)(2,1)S(1)}, bf16[192,1536]{1,0:T(8,128)(2,1)S(1)}, u32[]{:S(2)}, u32[]{:S(2)}) collective-permute-start(bf16[192,1536]{1,0:T(8,128)(2,1)S(1)} %collective-permute-done.13.rest_10_.rest_7_), channel_id=1, source_target_pairs={{0,4},{2,6},{4,0},{6,2},{8,12},{10,14},{12,8},{14,10},{16,20},{18,... | collective-permute-start | bytes 1769480 | tf_op jit(solution)/shard_map/ppermute | solution.py:880
  57.5 38.1 %collective-permute-start.11 = (bf16[240,1536]{1,0:T(8,128)(2,1)S(1)}, bf16[240,1536]{1,0:T(8,128)(2,1)S(1)}, u32[]{:S(2)}, u32[]{:S(2)}) collective-permute-start(bf16[240,1536]{1,0:T(8,128)(2,1)S(1)} %collective-permute-done.9.rest_6_.rest_3_), channel_id=1, source_target_pairs={{0,2},{2,0},{4,6},{6,4},{8,10},{10,8},{12,14},{14,12},{16,18},{18,... | collective-permute-start | bytes 2211848 | tf_op jit(solution)/shard_map/ppermute | solution.py:880
  153.8 41.8 %collective-permute-start.17 = (bf16[2,1536,384]{2,1,0:T(8,128)(2,1)}, bf16[2,1536,384]{2,1,0:T(8,128)(2,1)S(1)}, u32[]{:S(2)}, u32[]{:S(2)}) collective-permute-start(bf16[2,1536,384]{2,1,0:T(8,128)(2,1)} %get-tuple-element.132), channel_id=1, source_target_pairs={{0,2},{2,0},{4,6},{6,4},{8,10},{10,8},{12,14},{14,12},{16,18},{18,... | collective-permute-start | bytes 7077896 | tf_op jit(solution)/shard_map/ppermute | solution.py:880
  211.7 30.1 %collective-permute-start.19 = (bf16[2,496,1536]{2,1,0:T(8,128)(2,1)}, bf16[2,496,1536]{2,1,0:T(8,128)(2,1)S(1)}, u32[]{:S(2)}, u32[]{:S(2)}) collective-permute-start(bf16[2,496,1536]{2,1,0:T(8,128)(2,1)} %get-tuple-element.157), channel_id=1, source_target_pairs={{0,2},{2,0},{4,6},{6,4},{8,10},{10,8},{12,14},{14,12},{16,18},{18,... | collective-permute-start | bytes 9142280 | tf_op jit(solution)/shard_map/ppermute | solution.py:880
  211.8 28.8 %collective-permute-start.18 = (bf16[1536,384]{1,0:T(8,128)(2,1)S(1)}, bf16[1536,384]{1,0:T(8,128)(2,1)S(1)}, u32[]{:S(2)}, u32[]{:S(2)}) collective-permute-start(bf16[1536,384]{1,0:T(8,128)(2,1)S(1)} %get-tuple-element.220), channel_id=1, source_target_pairs={{0,1},{1,0},{2,3},{3,2},{4,5},{5,4},{6,7},{7,6},{8,9},{9,8},{10,11... | collective-permute-start | bytes 3538952 | tf_op jit(solution)/shard_map/ppermute | solution.py:884
  254.1 36.2 %collective-permute-start.23 = (bf16[496,1536]{1,0:T(8,128)(2,1)S(1)}, bf16[496,1536]{1,0:T(8,128)(2,1)S(1)}, u32[]{:S(2)}, u32[]{:S(2)}) collective-permute-start(bf16[496,1536]{1,0:T(8,128)(2,1)S(1)} %get-tuple-element.218), channel_id=1, source_target_pairs={{0,1},{1,0},{2,3},{3,2},{4,5},{5,4},{6,7},{7,6},{8,9},{9,8},{10,11... | collective-permute-start | bytes 4571144 | tf_op jit(solution)/shard_map/ppermute | solution.py:884
  273.3 48.3 %collective-permute-start.28 = (bf16[400,768]{1,0:T(8,128)(2,1)}, bf16[400,768]{1,0:T(8,128)(2,1)}, u32[]{:S(2)}, u32[]{:S(2)}) collective-permute-start(bf16[400,768]{1,0:T(8,128)(2,1)} %get-tuple-element.228), channel_id=1, source_target_pairs={{0,1},{1,0},{2,3},{3,2},{4,5},{5,4},{6,7},{7,6},{8,9},{9,8},{10,11... | collective-permute-start | bytes 1843208 | tf_op jit(solution)/shard_map/ppermute | solution.py:884
  284.4 26.7 %collective-permute-start.25 = (bf16[2,400,768]{2,1,0:T(8,128)(2,1)}, bf16[2,400,768]{2,1,0:T(8,128)(2,1)S(1)}, u32[]{:S(2)}, u32[]{:S(2)}) collective-permute-start(bf16[2,400,768]{2,1,0:T(8,128)(2,1)} %get-tuple-element.171), channel_id=1, source_target_pairs={{0,2},{2,0},{4,6},{6,4},{8,10},{10,8},{12,14},{14,12},{16,18},{18,... | collective-permute-start | bytes 3686408 | tf_op jit(solution)/shard_map/ppermute | solution.py:880
  291.5 29.6 %collective-permute-start.26 = (bf16[768,384]{1,0:T(8,128)(2,1)S(1)}, bf16[768,384]{1,0:T(8,128)(2,1)S(1)}, u32[]{:S(2)}, u32[]{:S(2)}) collective-permute-start(bf16[768,384]{1,0:T(8,128)(2,1)S(1)} %add_convert_fusion.16), channel_id=1, source_target_pairs={{0,16},{2,18},{4,20},{6,22},{8,24},{10,26},{12,28},{14,30},{16,0},... | collective-permute-start | bytes 1769480 | tf_op jit(solution)/shard_map/ppermute | solution.py:880
  309.0 26.6 %collective-permute-start.27 = (bf16[496,768]{1,0:T(8,128)(2,1)S(1)}, bf16[496,768]{1,0:T(8,128)(2,1)S(1)}, u32[]{:S(2)}, u32[]{:S(2)}) collective-permute-start(bf16[496,768]{1,0:T(8,128)(2,1)S(1)} %add_convert_fusion.6), channel_id=1, source_target_pairs={{0,8},{2,10},{4,12},{6,14},{8,0},{10,2},{12,4},{14,6},{16,24},{18,... | collective-permute-start | bytes 2285576 | tf_op jit(solution)/shard_map/ppermute | solution.py:880
  311.4 36.5 %collective-permute-start.31 = (bf16[400,768]{1,0:T(8,128)(2,1)S(1)}, bf16[400,768]{1,0:T(8,128)(2,1)S(1)}, u32[]{:S(2)}, u32[]{:S(2)}) collective-permute-start(bf16[400,768]{1,0:T(8,128)(2,1)S(1)} %get-tuple-element.226), channel_id=1, source_target_pairs={{0,1},{1,0},{2,3},{3,2},{4,5},{5,4},{6,7},{7,6},{8,9},{9,8},{10,11... | collective-permute-start | bytes 1843208 | tf_op jit(solution)/shard_map/ppermute | solution.py:884
  321.3 29.5 %collective-permute-start.33 = (bf16[768,384]{1,0:T(8,128)(2,1)S(1)}, bf16[768,384]{1,0:T(8,128)(2,1)}, u32[]{:S(2)}, u32[]{:S(2)}) collective-permute-start(bf16[768,384]{1,0:T(8,128)(2,1)S(1)} %add_convert_fusion.15.rest_0_), channel_id=1, source_target_pairs={{0,2},{2,0},{4,6},{6,4},{8,10},{10,8},{12,14},{14,12},{16,18},{18,... | collective-permute-start | bytes 1769480 | tf_op jit(solution)/shard_map/ppermute | solution.py:880
  321.3 25.1 %collective-permute-start.29 = (bf16[768,384]{1,0:T(8,128)(2,1)S(1)}, bf16[768,384]{1,0:T(8,128)(2,1)}, u32[]{:S(2)}, u32[]{:S(2)}) collective-permute-start(bf16[768,384]{1,0:T(8,128)(2,1)S(1)} %add_convert_fusion.15.rest_0_), channel_id=1, source_target_pairs={{0,4},{2,6},{4,0},{6,2},{8,12},{10,14},{12,8},{14,10},{16,20},{18,... | collective-permute-start | bytes 1769480 | tf_op jit(solution)/shard_map/ppermute | solution.py:880
  321.6 35.2 %collective-permute-start.32 = (bf16[2,400,768]{2,1,0:T(8,128)(2,1)}, bf16[2,400,768]{2,1,0:T(8,128)(2,1)S(1)}, u32[]{:S(2)}, u32[]{:S(2)}) collective-permute-start(bf16[2,400,768]{2,1,0:T(8,128)(2,1)} %get-tuple-element.180), channel_id=1, source_target_pairs={{0,2},{2,0},{4,6},{6,4},{8,10},{10,8},{12,14},{14,12},{16,18},{18,... | collective-permute-start | bytes 3686408 | tf_op jit(solution)/shard_map/ppermute | solution.py:880
  346.5 43.7 %collective-permute-start.35 = (bf16[496,768]{1,0:T(8,128)(2,1)S(1)}, bf16[496,768]{1,0:T(8,128)(2,1)S(1)}, u32[]{:S(2)}, u32[]{:S(2)}) collective-permute-start(bf16[496,768]{1,0:T(8,128)(2,1)S(1)} %add_convert_fusion.5), channel_id=1, source_target_pairs={{0,16},{2,18},{4,20},{6,22},{8,24},{10,26},{12,28},{14,30},{16,0},... | collective-permute-start | bytes 2285576 | tf_op jit(solution)/shard_map/ppermute | solution.py:880
  348.0 23.4 %collective-permute-start.36 = (bf16[400,384]{1,0:T(8,128)(2,1)S(1)}, bf16[400,384]{1,0:T(8,128)(2,1)S(1)}, u32[]{:S(2)}, u32[]{:S(2)}) collective-permute-start(bf16[400,384]{1,0:T(8,128)(2,1)S(1)} %add_convert_fusion.30), channel_id=1, source_target_pairs={{0,8},{2,10},{4,12},{6,14},{8,0},{10,2},{12,4},{14,6},{16,24},{18,... | collective-permute-start | bytes 921608 | tf_op jit(solution)/shard_map/ppermute | solution.py:880
  357.2 33.2 %collective-permute-start.38 = (bf16[400,768]{1,0:T(8,128)(2,1)S(1)}, bf16[400,768]{1,0:T(8,128)(2,1)S(1)}, u32[]{:S(2)}, u32[]{:S(2)}) collective-permute-start(bf16[400,768]{1,0:T(8,128)(2,1)S(1)} %get-tuple-element.224), channel_id=1, source_target_pairs={{0,1},{1,0},{2,3},{3,2},{4,5},{5,4},{6,7},{7,6},{8,9},{9,8},{10,11... | collective-permute-start | bytes 1843208 | tf_op jit(solution)/shard_map/ppermute | solution.py:884
  371.5 32.8 %collective-permute-start.42 = (bf16[400,384]{1,0:T(8,128)(2,1)S(1)}, bf16[400,384]{1,0:T(8,128)(2,1)S(1)}, u32[]{:S(2)}, u32[]{:S(2)}) collective-permute-start(bf16[400,384]{1,0:T(8,128)(2,1)S(1)} %add_convert_fusion.27), channel_id=1, source_target_pairs={{0,16},{2,18},{4,20},{6,22},{8,24},{10,26},{12,28},{14,30},{16,0},... | collective-permute-start | bytes 921608 | tf_op jit(solution)/shard_map/ppermute | solution.py:880
  404.3 31.8 %collective-permute-start.40 = (bf16[496,768]{1,0:T(8,128)(2,1)S(1)}, bf16[496,768]{1,0:T(8,128)(2,1)S(1)}, u32[]{:S(2)}, u32[]{:S(2)}) collective-permute-start(bf16[496,768]{1,0:T(8,128)(2,1)S(1)} %add_convert_fusion.4.rest_0_), channel_id=1, source_target_pairs={{0,2},{2,0},{4,6},{6,4},{8,10},{10,8},{12,14},{14,12},{16,18},{18,... | collective-permute-start | bytes 2285576 | tf_op jit(solution)/shard_map/ppermute | solution.py:880
  404.4 24.2 %collective-permute-start.47 = (bf16[400,384]{1,0:T(8,128)(2,1)S(1)}, bf16[400,384]{1,0:T(8,128)(2,1)S(1)}, u32[]{:S(2)}, u32[]{:S(2)}) collective-permute-start(bf16[400,384]{1,0:T(8,128)(2,1)S(1)} %add_convert_fusion.22), channel_id=1, source_target_pairs={{0,16},{2,18},{4,20},{6,22},{8,24},{10,26},{12,28},{14,30},{16,0},... | collective-permute-start | bytes 921608 | tf_op jit(solution)/shard_map/ppermute | solution.py:880
  (86 other events, 937.9 us)
